TPU v7x, 128 devices: a whole 4x4x4 slice. The times are simulated.
128 devices in a mesh: gx: 16 (over y, x_hi, core), gy: 8 (over z, x_lo).
Axes of the slice: x: 4 (x_hi: 2, x_lo: 2; x = x_hi * 2 + x_lo), y: 4, z: 4, core: 2. Of those that a mesh axis runs over, the one named last changes fastest.
Arguments:
- slab_tokens: bfloat16 [32, 16, 32, 512], P('gx', None, 'gy'), may hold values from -6 to 6
- cotangent: bfloat16 [32, 16, 32, 512], P('gx', 'gy'), may hold values from -6 to 6
- w_qkv: bfloat16 [1536, 512], replicated, may hold values from -1 to 1
- w_out: bfloat16 [512, 512], replicated, may hold values from -0.75 to 0.75
- logit_scale: float32 [8], replicated, may hold values from 1 to 400
Outputs:
- output: bfloat16 [32, 16, 32, 512], P('gx', 'gy')
- grad_input: bfloat16 [32, 16, 32, 512], P('gx', None, 'gy')
- grad_weights: float32 [2048, 512], P(('gx', 'gy'))
All inputs are finite; a program needn't handle non-finite values.
Results may differ from a plain program's by a relative error of at most 0.011.
The roundings to bfloat16 on the way count: a program that leaves them out, or rounds other values in their place, can miss the bound.
Values may be sent and summed in bfloat16 or wider, within the bound.
A program may use at most 128 MiB of HBM per device.

v0:
```python
from functools import partial
import math

import jax
import jax.numpy as jnp
from jax import lax
from jax.sharding import PartitionSpec as P

D = 512
HEADS = 8
HEAD_DIM = 64


EPSILON = 1e-06
NEGATIVE = -1e30
OFFSETS = tuple(
    ((first, second, third) for first in range(3) for second in range(3) for third in range(3))
)


def shortened(x):
    return jax.tree.map(lambda a: a.astype(jnp.bfloat16) if a.dtype == jnp.float32 else a, x)


def extended(block, sides, width):
    for axis, dim in sides:
        count = lax.axis_size(axis)
        forward = [(i, i + 1) for i in range(count - 1)]
        backward = [(target, source) for source, target in forward]
        low = lax.ppermute(
            lax.slice_in_dim(block, block.shape[dim] - width, None, axis=dim), axis, forward
        )
        high = lax.ppermute(lax.slice_in_dim(block, 0, width, axis=dim), axis, backward)
        block = jnp.concatenate([low, block, high], axis=dim)
    return block


def rms_rows(values):
    return values * lax.rsqrt(jnp.mean(values * values, axis=-1, keepdims=True) + EPSILON)


def head_split(values):
    return values.reshape(values.shape[:-1] + (HEADS, HEAD_DIM))


def project_heads(qkv_all, logit_scale):
    leading = qkv_all.shape[:-1]
    query_part = rms_rows(head_split(qkv_all[..., :D])) * (logit_scale / HEAD_DIM)[:, None]
    key_part = rms_rows(head_split(qkv_all[..., D : 2 * D]))
    pairs = jnp.concatenate([key_part.reshape(leading + (D,)), qkv_all[..., 2 * D :]], axis=-1)
    return (query_part.reshape(leading + (D,)), pairs)


def offset_score(offset):

    def compute(queries, key_part):
        extent = queries.shape[:3]
        window = lax.slice(
            key_part,
            (offset[0], offset[1], offset[2], 0),
            (
                offset[0] + extent[0],
                offset[1] + extent[1],
                offset[2] + extent[2],
                key_part.shape[3],
            ),
        )
        return jnp.sum(head_split(queries) * head_split(window), axis=-1)

    return jax.checkpoint(compute)


def offset_mix(offset):

    def compute(weights, value_part):
        extent = weights.shape[:3]
        window = lax.slice(
            value_part,
            (offset[0], offset[1], offset[2], 0),
            (
                offset[0] + extent[0],
                offset[1] + extent[1],
                offset[2] + extent[2],
                value_part.shape[3],
            ),
        )
        return (weights[..., None] * head_split(window)).reshape(extent + (D,))

    return jax.checkpoint(compute)


def attend(queries, kv_ext, start_x, start_y, total_x, total_y):
    extent = queries.shape[:3]
    key_part = kv_ext[..., :D]
    value_part = kv_ext[..., D:]
    pos_x = start_x + lax.iota(jnp.int32, extent[0])
    pos_y = start_y + lax.iota(jnp.int32, extent[1])
    pos_z = lax.iota(jnp.int32, extent[2])
    scores = []
    for offset in OFFSETS:
        flag_x = (pos_x + offset[0] - 1 >= 0) & (pos_x + offset[0] - 1 < total_x)
        flag_y = (pos_y + offset[1] - 1 >= 0) & (pos_y + offset[1] - 1 < total_y)
        flag_z = (pos_z + offset[2] - 1 >= 0) & (pos_z + offset[2] - 1 < extent[2])
        inside = (
            flag_x[:, None, None, None] & flag_y[None, :, None, None] & flag_z[None, None, :, None]
        )
        scores.append(jnp.where(inside, offset_score(offset)(queries, key_part), NEGATIVE))
    stacked = jnp.stack(scores)
    weights = jax.nn.softmax(stacked, axis=0)
    log_totals = jax.nn.logsumexp(stacked, axis=0)
    blended = jnp.zeros(extent + (D,), queries.dtype)
    for index, offset in enumerate(OFFSETS):
        blended = blended + offset_mix(offset)(weights[index], value_part)
    return (blended, log_totals)


def fold_rims(grad_ext):
    size_x = grad_ext.shape[0] - 2
    size_y = grad_ext.shape[1] - 2
    beside_all = extended(shortened(grad_ext), (("gx", 0), ("gy", 1)), 1).astype(grad_ext.dtype)
    total = beside_all[2 : size_x + 2, 2 : size_y + 2]
    total = total.at[0].add(beside_all[0, 2 : size_y + 2])
    total = total.at[size_x - 1].add(beside_all[size_x + 3, 2 : size_y + 2])
    total = total.at[:, 0].add(beside_all[2 : size_x + 2, 0])
    total = total.at[:, size_y - 1].add(beside_all[2 : size_x + 2, size_y + 3])
    total = total.at[0, 0].add(beside_all[0, 0])
    total = total.at[0, size_y - 1].add(beside_all[0, size_y + 3])
    total = total.at[size_x - 1, 0].add(beside_all[size_x + 3, 0])
    total = total.at[size_x - 1, size_y - 1].add(beside_all[size_x + 3, size_y + 3])
    return total


def on_device(slab_tokens, cotangent, w_qkv, w_out, logit_scale):
    blocks = lax.all_to_all(slab_tokens, "gy", split_axis=1, concat_axis=2, tiled=True)
    size_x, size_y, size_z = blocks.shape[:3]
    total_x = size_x * lax.axis_size("gx")
    total_y = size_y * lax.axis_size("gy")
    start_x = lax.axis_index("gx") * size_x
    start_y = lax.axis_index("gy") * size_y
    x_float = blocks.astype(jnp.float32)
    normed_float, norm_back = jax.vjp(rms_rows, x_float)
    normed_rows = normed_float.astype(jnp.bfloat16).reshape(-1, D)
    qkv_all = jnp.dot(normed_rows, w_qkv.T, preferred_element_type=jnp.float32).reshape(
        size_x, size_y, size_z, 3 * D
    )
    (query_float, pair_float), head_back = jax.vjp(
        partial(project_heads, logit_scale=logit_scale), qkv_all
    )
    query_b = query_float.astype(jnp.bfloat16)
    pair_b = pair_float.astype(jnp.bfloat16)
    pair_rims = extended(pair_b, (("gx", 0), ("gy", 1)), 1)
    kv_ext = jnp.pad(pair_rims, ((0, 0), (0, 0), (1, 1), (0, 0))).astype(jnp.float32)
    attend_here = partial(
        attend, start_x=start_x, start_y=start_y, total_x=total_x, total_y=total_y
    )
    attended, attention_back, log_totals = jax.vjp(
        attend_here, query_b.astype(jnp.float32), kv_ext, has_aux=True
    )
    attended_rows = attended.astype(jnp.bfloat16).reshape(-1, D)
    projected = jnp.dot(attended_rows, w_out.T, preferred_element_type=jnp.float32)
    block_out = (x_float + projected.reshape(x_float.shape)).astype(jnp.bfloat16)
    grad_rows = cotangent.reshape(-1, D)
    upstream = (
        jnp.dot(grad_rows, w_out, preferred_element_type=jnp.float32)
        .astype(jnp.bfloat16)
        .reshape(x_float.shape)
    )
    upstream_float = upstream.astype(jnp.float32)
    grad_query, grad_ext = attention_back(upstream_float)
    grad_kv = fold_rims(grad_ext[:, :, 1:-1])
    (grad_qkv,) = head_back((grad_query, grad_kv))
    grad_qkv_b = grad_qkv.astype(jnp.bfloat16).reshape(-1, 3 * D)
    grad_normed = jnp.dot(grad_qkv_b, w_qkv, preferred_element_type=jnp.float32).reshape(
        x_float.shape
    )
    (grad_norm_in,) = norm_back(grad_normed)
    grad_block = (cotangent.astype(jnp.float32) + grad_norm_in).astype(jnp.bfloat16)
    grad_input = lax.all_to_all(grad_block, "gy", split_axis=2, concat_axis=1, tiled=True)
    factor = 1.0 / math.sqrt(size_x * size_y * size_z * lax.axis_size("gx") * lax.axis_size("gy"))
    grad_first = jnp.dot(grad_qkv_b.T, normed_rows, preferred_element_type=jnp.float32) * factor
    grad_second = jnp.dot(grad_rows.T, attended_rows, preferred_element_type=jnp.float32) * factor
    grad_weights = lax.psum_scatter(
        jnp.concatenate([grad_first, grad_second], axis=0),
        ("gx", "gy"),
        scatter_dimension=0,
        tiled=True,
    )
    return (block_out, grad_input, grad_weights)


def solution(mesh):
    return jax.shard_map(
        on_device,
        mesh=mesh,
        in_specs=(P("gx", None, "gy", None), P("gx", "gy", None, None), P(), P(), P()),
        out_specs=(P("gx", "gy", None, None), P("gx", None, "gy", None), P(("gx", "gy"), None)),
        check_vma=False,
    )
```

profile of v0, /device:TPU:0, one launch (start us, length us, event | category | flops | bytes accessed | tf_op | source)
XLA Modules:
  0.0 1360.4 jit_solution(10644671636160407080)
XLA Ops:
  8.9 6.3 all-to-all-start
  16.7 2.0 convolution_convert_fusion
  19.4 2.5 all-to-all-done
  32.7 4.2 collective-permute-done.1
  37.0 2.1 collective-permute-start.2
  42.9 6.4 collective-permute-done.3
  53.0 2.3 convert_multiply_fusion
  319.1 2.0 fusion.121
  334.2 2.2 mul.1570
  437.7 2.5 multiply_reduce_fusion
  559.7 2.0 mul.1493
  615.8 2.0 mul.1521
  627.6 2.0 mul.1505
  635.3 4.7 multiply_add_fusion
  644.9 5.9 collective-permute-start.4
  652.4 9.4 fusion.27
  662.8 3.5 collective-permute-start.6
  673.4 2.3 fusion.7
  675.7 7.1 collective-permute-done.7
  687.2 2.1 fusion.56
  701.6 2.4 pad_maximum_fusion
  706.9 4.9 all-to-all-start.1
  712.8 6.1 all-to-all-done.1
  719.6 633.7 %reduce-scatter.2.cloned.1.call-done = f32[16,512]{1,0:T(8,128)} async-done(((f32[2048,512]{1,0:T(8,128)}), f32[16,512]{1,0:T(8,128)}) %reduce-scatter.2.cloned.1.call-update) | async-done | bytes 32784 | tf_op jit(solution)/shard_map/reduce_scatter | solution.py:182
  (838 shorter events, 623.0 us)
Async XLA Ops:
  8.9 13.0 all-to-all-start
  15.2 1338.1 %reduce-scatter.2.cloned.1.call-start = ((), (), s32[]{:S(2)}) async-start(), calls=%async_computation.3 | async-start | bytes 4227072 | tf_op jit(solution)/shard_map/reduce_scatter | solution.py:182
  29.4 3.3 collective-permute-start
  30.7 6.2 collective-permute-start.1
  37.0 5.9 collective-permute-start.2
  39.0 10.3 collective-permute-start.3
  61.6 110.7 %copy-start.104 = (f32[2,2,32,8]{3,2,1,0:T(8,128)}, f32[2,2,32,8]{3,2,1,0:T(8,128)S(1)}, u32[]{:S(2)}) copy-start(f32[2,2,32,8]{3,2,1,0:T(8,128)S(1)} %reduce_sum.778) | copy-start | bytes 12292
  155.9 21.9 %copy-start.107 = (f32[2,2,32,8]{3,2,1,0:T(8,128)S(1)}, f32[2,2,32,8]{3,2,1,0:T(8,128)}, u32[]{:S(2)}) copy-start(f32[2,2,32,8]{3,2,1,0:T(8,128)} %reduce_sum.794) | copy-start | bytes 12292
  155.9 21.9 %copy-start.112 = (f32[2,2,32,8]{3,2,1,0:T(8,128)S(1)}, f32[2,2,32,8]{3,2,1,0:T(8,128)}, u32[]{:S(2)}) copy-start(f32[2,2,32,8]{3,2,1,0:T(8,128)} %reduce_sum.646) | copy-start | bytes 12292
  155.9 21.9 %copy-start.113 = (f32[2,2,32,8]{3,2,1,0:T(8,128)S(1)}, f32[2,2,32,8]{3,2,1,0:T(8,128)}, u32[]{:S(2)}) copy-start(f32[2,2,32,8]{3,2,1,0:T(8,128)} %reduce_sum.744) | copy-start | bytes 12292
  155.9 21.9 %copy-start.114 = (f32[2,2,32,8]{3,2,1,0:T(8,128)S(1)}, f32[2,2,32,8]{3,2,1,0:T(8,128)}, u32[]{:S(2)}) copy-start(f32[2,2,32,8]{3,2,1,0:T(8,128)} %reduce_sum.746) | copy-start | bytes 12292
  155.9 21.9 %copy-start.115 = (f32[2,2,32,8]{3,2,1,0:T(8,128)S(1)}, f32[2,2,32,8]{3,2,1,0:T(8,128)}, u32[]{:S(2)}) copy-start(f32[2,2,32,8]{3,2,1,0:T(8,128)} %reduce_sum.748) | copy-start | bytes 12292
  155.9 21.9 %copy-start.116 = (f32[2,2,32,8]{3,2,1,0:T(8,128)S(1)}, f32[2,2,32,8]{3,2,1,0:T(8,128)}, u32[]{:S(2)}) copy-start(f32[2,2,32,8]{3,2,1,0:T(8,128)} %reduce_sum.750) | copy-start | bytes 12292
  155.9 21.9 %copy-start.117 = (f32[2,2,32,8]{3,2,1,0:T(8,128)S(1)}, f32[2,2,32,8]{3,2,1,0:T(8,128)}, u32[]{:S(2)}) copy-start(f32[2,2,32,8]{3,2,1,0:T(8,128)} %reduce_sum.752) | copy-start | bytes 12292
  155.9 21.9 %copy-start.118 = (f32[2,2,32,8]{3,2,1,0:T(8,128)S(1)}, f32[2,2,32,8]{3,2,1,0:T(8,128)}, u32[]{:S(2)}) copy-start(f32[2,2,32,8]{3,2,1,0:T(8,128)} %reduce_sum.754) | copy-start | bytes 12292
  155.9 21.9 %copy-start.119 = (f32[2,2,32,8]{3,2,1,0:T(8,128)S(1)}, f32[2,2,32,8]{3,2,1,0:T(8,128)}, u32[]{:S(2)}) copy-start(f32[2,2,32,8]{3,2,1,0:T(8,128)} %reduce_sum.756) | copy-start | bytes 12292
  156.0 21.9 %copy-start.120 = (f32[2,2,32,8]{3,2,1,0:T(8,128)S(1)}, f32[2,2,32,8]{3,2,1,0:T(8,128)}, u32[]{:S(2)}) copy-start(f32[2,2,32,8]{3,2,1,0:T(8,128)} %reduce_sum.758) | copy-start | bytes 12292
  156.0 21.9 %copy-start.121 = (f32[2,2,32,8]{3,2,1,0:T(8,128)S(1)}, f32[2,2,32,8]{3,2,1,0:T(8,128)}, u32[]{:S(2)}) copy-start(f32[2,2,32,8]{3,2,1,0:T(8,128)} %reduce_sum.760) | copy-start | bytes 12292
  156.0 21.9 %copy-start.122 = (f32[2,2,32,8]{3,2,1,0:T(8,128)S(1)}, f32[2,2,32,8]{3,2,1,0:T(8,128)}, u32[]{:S(2)}) copy-start(f32[2,2,32,8]{3,2,1,0:T(8,128)} %reduce_sum.762) | copy-start | bytes 12292
  644.9 16.9 %collective-permute-start.4 = (bf16[1,4,32,1024]{3,2,1,0:T(8,128)(2,1)}, bf16[1,4,32,1024]{3,2,1,0:T(8,128)(2,1)S(1)}, u32[]{:S(2)}, u32[]{:S(2)}) collective-permute-start(bf16[1,4,32,1024]{3,2,1,0:T(8,128)(2,1)} %get-tuple-element.454), channel_id=1, source_target_pairs={{0,8},{8,16},{16,24},{24,32},{32,40},{40,48},{48,56},{56,64},{64,7... | collective-permute-start | bytes 786440 | tf_op jit(solution)/shard_map/ppermute | solution.py:30
  650.8 11.0 collective-permute-start.5
  662.8 12.9 collective-permute-start.6
  666.3 16.5 %collective-permute-start.7 = (bf16[6,1,32,1024]{3,2,1,0:T(8,128)(2,1)}, bf16[6,1,32,1024]{3,2,1,0:T(8,128)(2,1)}, u32[]{:S(2)}, u32[]{:S(2)}) collective-permute-start(bf16[6,1,32,1024]{3,2,1,0:T(8,128)(2,1)} %get-tuple-element.513), channel_id=1, source_target_pairs={{1,0},{2,1},{3,2},{4,3},{5,4},{6,5},{7,6},{9,8},{10,9},{11,10},{12... | collective-permute-start | bytes 1179656 | tf_op jit(solution)/shard_map/ppermute | solution.py:33
  706.9 12.0 all-to-all-start.1
  (179 other events, 1125.9 us)
Sparse Core Ops, SparseCore 0:
  704.2 649.0 reduce-scatter.1
where the time goes:
time: 1380 us; the launch traced here: 1360 us
  waiting for transfers between devices  661 us (48%)
  local copies, waits for them, and re-layouts  416 us (30%)
  other arithmetic  230 us (17%)
  starting transfers between devices  29.6 us (2%)
  between operations  16.9 us (1%)
    reduce_scatter x1, waiting for transfers between devices, on_device(): lax.psum_scatter(jnp.concatenate([grad_first, grad_second], axis=0), ('gx...  634 us
    mul x137, local copies, waits for them, and re-layouts, compute(): return (weights[..., None] * head_split(window)).reshape(extent + (D,))  233 us
    broadcast_in_dim x54, local copies, waits for them, and re-layouts, compute(): return jnp.sum(head_split(queries) * head_split(window), axis=-1)  98.3 us
    mul x27, other arithmetic, compute(): return (weights[..., None] * head_split(window)).reshape(extent + (D,))  51.9 us
    mul x27, local copies, waits for them, and re-layouts, compute(): return jnp.sum(head_split(queries) * head_split(window), axis=-1)  51 us
    reduce_sum x27, other arithmetic, compute(): return (weights[..., None] * head_split(window)).reshape(extent + (D,))  50 us
    reduce_sum x27, other arithmetic, compute(): return jnp.sum(head_split(queries) * head_split(window), axis=-1)  49.4 us
  transfers between devices with their start and end apart: 11, of which 7 were waited for; matrix products, arithmetic and copies ran while one was open for 2% of the time, Pallas kernels for 0%

commit v1 on v0

v1 whole, which is shorter than its diff:
```python
import functools

import jax
import jax.numpy as jnp
from jax import lax
from jax.experimental import pallas as pl
from jax.experimental.pallas import tpu as pltpu
from jax.sharding import PartitionSpec as P

MESH = pl.DeviceIdType.MESH
F32 = jnp.float32
BF16 = jnp.bfloat16

D = 512
HEADS = 8
HEAD_DIM = 64
NX, NY, NZ = 32, 16, 32
GX, GY = 16, 8
CHIPS = 64
OWN = 128
EXT = 384
EPSILON = 1e-06
NEGATIVE = -1e30
FACTOR = 1.0 / 128.0

SIDES = ((-1, 0), (1, 0), (0, -1), (0, 1), (-1, -1), (-1, 1), (1, -1), (1, 1))
REGION = {
    (-1, 0): (8, 4),
    (1, 0): (12, 4),
    (0, -1): (16, 2),
    (0, 1): (18, 2),
    (-1, -1): (20, 1),
    (-1, 1): (21, 1),
    (1, -1): (22, 1),
    (1, 1): (23, 1),
}


def dot_nn(a, b):
    return jnp.dot(a, b, preferred_element_type=F32)


def dot_nt(a, b):
    return lax.dot_general(a, b, (((1,), (1,)), ((), ())), preferred_element_type=F32)


def dot_tn(a, b):
    return lax.dot_general(a, b, (((0,), (0,)), ((), ())), preferred_element_type=F32)


def iota(shape, dim):
    return lax.broadcasted_iota(jnp.int32, shape, dim)


def natural_row(r):
    return ((r >> 3) & 1) * 64 + (r & 1) * 32 + (r >> 4) * 4 + ((r >> 1) & 3)


def token_row(r):
    return ((r >> 3) & 1) * 64 + ((r >> 1) & 3) * 16 + (r >> 4) * 2 + (r & 1)


def slab_row(t):
    return ((t >> 6) & 1) * 64 + (t & 15) * 4 + ((t >> 4) & 3)


def gather_rows(index):
    shape = (OWN, OWN)
    return jnp.where(index(iota(shape, 0)) == iota(shape, 1), 1.0, 0.0).astype(BF16)


def scatter_rows(index):
    shape = (OWN, OWN)
    return jnp.where(index(iota(shape, 1)) == iota(shape, 0), 1.0, 0.0).astype(BF16)


def moved(matrix, rows):
    return dot_nn(matrix, rows).astype(BF16)


def neighbourhood_bias(gx, gy):
    shape = (EXT, OWN)
    row, col = iota(shape, 0), iota(shape, 1)
    cell, y = row >> 4, row & 15
    x = jnp.where(
        cell < 8,
        cell >> 2,
        jnp.where(
            cell < 16,
            jnp.where(cell < 12, -1, 2),
            jnp.where(cell < 20, cell & 1, jnp.where(cell < 22, -1, 2)),
        ),
    )
    z = jnp.where(
        cell < 16,
        cell & 3,
        jnp.where(
            cell < 20, jnp.where(cell < 18, -1, 4), jnp.where((cell & 1) == 0, -1, 4)
        ),
    )
    near = (
        (jnp.abs(x - (col >> 6)) <= 1)
        & (jnp.abs(z - ((col >> 4) & 3)) <= 1)
        & (jnp.abs(y - (col & 15)) <= 1)
    )
    full_x, full_z = x + 2 * gx, z + 4 * gy
    inside = (full_x >= 0) & (full_x < NX) & (full_z >= 0) & (full_z < NZ)
    return jnp.where(near & inside, 0.0, NEGATIVE)


def kernel(
    xs, cot, wqkv_hbm, wout_hbm, scale,
    out, gin, gw,
    xext, cot_send, cot_stage, wqkv, wout, normed, raw,
    q_b, k_b, v_b, q_hat, k_hat, q_inv, k_inv, u_b, att,
    gq, gk, gv, cot_tok, cot_t, bias,
    pair_send, pair_recv, half, sum_send, sum_recv,
    gn_send, gn_recv, out_send, out_stage,
    w_sem, x_ssem, x_rsem, c_ssem, c_rsem, p_ssem, p_rsem,
    a_ssem, a_rsem, g_ssem, g_rsem, o_ssem, o_rsem,
):
    gx, gy = lax.axis_index("gx"), lax.axis_index("gy")
    core = gx & 1
    chip = (gx >> 1) * GY + gy

    def exists(side):
        ok = None
        for at, step, size in ((gx, side[0], GX), (gy, side[1], GY)):
            if step:
                here = at > 0 if step < 0 else at < size - 1
                ok = here if ok is None else ok & here
        return ok

    def remote(src, dst, ssem, rsem, to_x, to_y):
        return pltpu.make_async_remote_copy(
            src_ref=src, dst_ref=dst, send_sem=ssem, recv_sem=rsem,
            device_id=(to_x, to_y), device_id_type=MESH,
        )

    def wait_for(ref, sem):
        pltpu.make_async_copy(ref, ref, sem).wait()

    load_qkv = pltpu.make_async_copy(wqkv_hbm, wqkv, w_sem.at[0])
    load_out = pltpu.make_async_copy(wout_hbm, wout, w_sem.at[1])
    load_qkv.start()
    load_out.start()

    barrier = pltpu.get_barrier_semaphore()

    def greet(k, carry):
        other = (chip + k) & (CHIPS - 1)
        pl.semaphore_signal(
            barrier, inc=1,
            device_id=((other >> 3) * 2 + core, other & 7), device_id_type=MESH,
        )
        return carry

    for side in SIDES:
        if side[0]:
            @pl.when(exists(side))
            def _():
                pl.semaphore_signal(
                    barrier, inc=1,
                    device_id=(gx + side[0], gy + side[1]), device_id_type=MESH,
                )
    lax.fori_loop(1, CHIPS, greet, 0)

    cot_send[...] = moved(gather_rows(natural_row), cot[...]).reshape(8, 16, D)
    one = jnp.int32(1)
    zero = jnp.int32(0)
    count_x = jnp.where(gx > 0, one, zero) + jnp.where(gx < GX - 1, one, zero)
    count_y = one + jnp.where(gy > 0, one, zero) + jnp.where(gy < GY - 1, one, zero)
    pl.semaphore_wait(barrier, (CHIPS - 1) + count_x * count_y)

    def border(ref, side):
        x = {-1: 0, 1: 1}.get(side[0])
        z = {-1: 0, 1: 3}.get(side[1])
        if z is None:
            return ref.at[x]
        if x is None:
            return ref.at[:, z]
        return ref.at[pl.ds(x, 1), z]

    def halo_copy(index, side):
        start, size = REGION[(-side[0], -side[1])]
        return remote(
            border(xs, side), xext.at[pl.ds(start, size)],
            x_ssem.at[index], x_rsem.at[index], gx + side[0], gy + side[1],
        )

    for index, side in enumerate(SIDES):
        @pl.when(exists(side))
        def _():
            halo_copy(index, side).start()

    def cot_copy(k, carry):
        to = (gy + k) & (GY - 1)
        remote(
            cot_send.at[to], cot_stage.at[gy], c_ssem.at[0], c_rsem.at[0], gx, to
        ).start()
        return carry

    lax.fori_loop(1, GY, cot_copy, 0)
    cot_stage[gy] = cot_send[gy]

    for side in SIDES:
        start, size = REGION[side]

        @pl.when(jnp.logical_not(exists(side)))
        def _():
            xext[pl.ds(start, size)] = jnp.zeros((size, 16, D), BF16)
            gn_recv[pl.ds(start - 8, size)] = jnp.zeros((size, 16, D), BF16)

    bias[...] = neighbourhood_bias(gx, gy)

    def rows_normed(rows):
        return rows * lax.rsqrt(jnp.mean(rows * rows, axis=-1, keepdims=True) + EPSILON)

    x_rows = xs[...].reshape(OWN, D)
    normed[0:OWN] = rows_normed(x_rows.astype(F32)).astype(BF16)
    load_qkv.wait()
    raw[:, 0:OWN] = dot_nt(wqkv[...], normed[0:OWN])

    def head_rows(base, h):
        return pl.ds(pl.multiple_of(base + h * HEAD_DIM, HEAD_DIM), HEAD_DIM)

    def head_inverse(values):
        return lax.rsqrt(jnp.mean(values * values, axis=0, keepdims=True) + EPSILON)

    def own_heads(h, carry):
        q = raw[head_rows(0, h), 0:OWN]
        inverse = head_inverse(q)
        hat = q * inverse
        q_hat[h] = hat
        q_inv[h] = inverse
        q_b[h] = (hat * (scale[h] / HEAD_DIM)).astype(BF16)
        k = raw[head_rows(D, h), 0:OWN]
        inverse = head_inverse(k)
        hat = k * inverse
        k_hat[h, :, 0:OWN] = hat
        k_inv[h, :, 0:OWN] = inverse
        k_b[h, :, 0:OWN] = hat.astype(BF16)
        v_b[h, :, 0:OWN] = raw[head_rows(2 * D, h), 0:OWN].astype(BF16)
        return carry

    lax.fori_loop(0, HEADS, own_heads, 0)

    load_out.wait()
    wait_for(cot_stage.at[pl.ds(0, GY - 1)], c_rsem.at[0])
    tokens = moved(scatter_rows(token_row), cot_stage[...].reshape(OWN, D))
    cot_tok[...] = tokens
    cot_t[...] = tokens.T.reshape(8, HEAD_DIM, OWN)
    u_b[...] = (
        dot_tn(wout[...], cot_t[...].reshape(D, OWN))
        .astype(BF16)
        .reshape(HEADS, HEAD_DIM, OWN)
    )

    for index, side in enumerate(SIDES):
        opposite = SIDES.index((-side[0], -side[1]))
        start, size = REGION[side]

        @pl.when(exists(side))
        def _():
            wait_for(xext.at[pl.ds(start, size)], x_rsem.at[opposite])

    halo_rows = xext[8:24].reshape(EXT - OWN, D)
    normed[OWN:EXT] = rows_normed(halo_rows.astype(F32)).astype(BF16)
    raw[D : 3 * D, OWN:EXT] = dot_nt(wqkv[D : 3 * D], normed[OWN:EXT])

    def halo_heads(h, carry):
        k = raw[head_rows(D, h), OWN:EXT]
        inverse = head_inverse(k)
        hat = k * inverse
        k_hat[h, :, OWN:EXT] = hat
        k_inv[h, :, OWN:EXT] = inverse
        k_b[h, :, OWN:EXT] = hat.astype(BF16)
        v_b[h, :, OWN:EXT] = raw[head_rows(2 * D, h), OWN:EXT].astype(BF16)
        return carry

    lax.fori_loop(0, HEADS, halo_heads, 0)

    def back_through(grad, hat, inverse):
        return inverse * (grad - hat * jnp.mean(grad * hat, axis=0, keepdims=True))

    def attend(h, carry):
        q, k, v, u = q_b[h], k_b[h], v_b[h], u_b[h]
        scores = dot_tn(k, q) + bias[...]
        shifted = jnp.exp(scores - jnp.max(scores, axis=0, keepdims=True))
        weights = shifted * (1.0 / jnp.sum(shifted, axis=0, keepdims=True))
        weights_b = weights.astype(BF16)
        att[h] = dot_nn(v, weights_b).astype(BF16)
        grad_w = dot_tn(v, u)
        inner = jnp.sum(weights * grad_w, axis=0, keepdims=True)
        grad_s = (weights * (grad_w - inner)).astype(BF16)
        grad_q = dot_nn(k, grad_s)
        gq[h] = (
            back_through(grad_q, q_hat[h], q_inv[h]) * (scale[h] / HEAD_DIM)
        ).astype(BF16)
        grad_k = dot_nt(q, grad_s)
        gk[h] = back_through(grad_k, k_hat[h], k_inv[h]).astype(BF16)
        gv[h] = dot_nt(u, weights_b).astype(BF16)
        return carry

    lax.fori_loop(0, HEADS, attend, 0)

    def weight_block(part, which, of_core):
        at = pl.ds((2 * which + of_core) * 2, 2)
        if part == 3:
            rows = cot_t[at].reshape(128, OWN)
            return dot_nt(rows, att[...].reshape(D, OWN))
        if part == 0:
            return dot_nn(gq[at].reshape(128, OWN), normed[0:OWN])
        return dot_nn((gk if part == 1 else gv)[at].reshape(128, EXT), normed[...])

    def pair_copy(part):
        return remote(
            pair_send.at[part], pair_recv.at[part],
            p_ssem.at[part], p_rsem.at[part], gx + 1 - 2 * core, gy,
        )

    order = (3, 0, 1, 2)
    for part in order:
        for which in range(2):
            pair_send[part, which] = weight_block(part, which, 1 - core).astype(BF16)
        pair_copy(part).start()
    for part in order:
        for which in range(2):
            half[part, which] = weight_block(part, which, core)

    grad_kv_halo = jnp.concatenate(
        [gk[:, :, OWN:EXT].reshape(D, EXT - OWN), gv[:, :, OWN:EXT].reshape(D, EXT - OWN)],
        axis=0,
    )
    gn_send[...] = (
        dot_tn(grad_kv_halo, wqkv[D : 3 * D]).astype(BF16).reshape(16, 16, D)
    )

    def grad_copy(index, side):
        start, size = REGION[side]
        target, _ = REGION[(-side[0], -side[1])]
        return remote(
            gn_send.at[pl.ds(start - 8, size)], gn_recv.at[pl.ds(target - 8, size)],
            g_ssem.at[index], g_rsem.at[index], gx + side[0], gy + side[1],
        )

    for index, side in enumerate(SIDES):
        @pl.when(exists(side))
        def _():
            grad_copy(index, side).start()

    for part in order:
        pair_copy(part).wait_recv()
        total = half[part] + pair_recv[part].astype(F32)
        sum_send[16 * part : 16 * part + 16] = total.astype(BF16).reshape(16, 16, D)

    def sum_copy(k, carry):
        other = (chip + k) & (CHIPS - 1)
        remote(
            sum_send.at[other], sum_recv.at[chip], a_ssem.at[0], a_rsem.at[0],
            (other >> 3) * 2 + core, other & 7,
        ).start()
        return carry

    lax.fori_loop(1, CHIPS, sum_copy, 0)
    sum_recv[chip] = sum_send[chip]

    projected = dot_nn(wout[...], att[...].reshape(D, OWN)).T
    out_rows = (x_rows.astype(F32) + projected).astype(BF16)
    out_send[...] = moved(gather_rows(token_row), out_rows).reshape(8, 16, D)

    def out_copy(k, carry):
        to = (gy + k) & (GY - 1)
        remote(
            out_send.at[to], out_stage.at[gy], o_ssem.at[0], o_rsem.at[0], gx, to
        ).start()
        return carry

    lax.fori_loop(1, GY, out_copy, 0)
    out_stage[gy] = out_send[gy]

    grad_own = jnp.concatenate(
        [
            gq[...].reshape(D, OWN),
            gk[:, :, 0:OWN].reshape(D, OWN),
            gv[:, :, 0:OWN].reshape(D, OWN),
        ],
        axis=0,
    )
    grad_n = dot_tn(grad_own, wqkv[...]).reshape(2, 4, 16, D)
    for index, side in enumerate(SIDES):
        opposite = SIDES.index((-side[0], -side[1]))
        start, size = REGION[side]

        @pl.when(exists(side))
        def _():
            wait_for(gn_recv.at[pl.ds(start - 8, size)], g_rsem.at[opposite])

    def term(side):
        start, size = REGION[side]
        return gn_recv[start - 8 : start - 8 + size].astype(F32)

    planes = []
    for x in range(2):
        side_x = (-1, 1)[x]
        plane = grad_n[x] + term((side_x, 0))
        low = term((0, -1))[x] + term((side_x, -1))[0]
        high = term((0, 1))[x] + term((side_x, 1))[0]
        planes.append(
            jnp.concatenate(
                [plane[0:1] + low[None], plane[1:3], plane[3:4] + high[None]], axis=0
            )
        )
    grad_n = jnp.concatenate(planes, axis=0).reshape(OWN, D)
    x_float = x_rows.astype(F32)
    inverse = lax.rsqrt(jnp.mean(x_float * x_float, axis=-1, keepdims=True) + EPSILON)
    x_hat = x_float * inverse
    grad_x = inverse * (grad_n - x_hat * jnp.mean(grad_n * x_hat, axis=-1, keepdims=True))
    grad_rows = (cot_tok[...].astype(F32) + grad_x).astype(BF16)
    gin[...] = moved(scatter_rows(slab_row), grad_rows)

    wait_for(out_stage.at[pl.ds(0, GY - 1)], o_rsem.at[0])
    out[...] = moved(scatter_rows(natural_row), out_stage[...].reshape(OWN, D))

    wait_for(sum_recv.at[pl.ds(0, CHIPS - 1)], a_rsem.at[0])
    gw[...] = jnp.sum(sum_recv[...].astype(F32), axis=0) * FACTOR

    for index, side in enumerate(SIDES):
        @pl.when(exists(side))
        def _():
            halo_copy(index, side).wait_send()
            grad_copy(index, side).wait_send()

    for part in order:
        pair_copy(part).wait_send()
    wait_for(cot_send.at[pl.ds(0, GY - 1)], c_ssem.at[0])
    wait_for(out_send.at[pl.ds(0, GY - 1)], o_ssem.at[0])
    wait_for(sum_send.at[pl.ds(0, CHIPS - 1)], a_ssem.at[0])


def on_device(slab_tokens, cotangent, w_qkv, w_out, logit_scale):
    xs = slab_tokens.transpose(0, 2, 1, 3)
    vmem = pl.BlockSpec(memory_space=pltpu.VMEM)
    hbm = pl.BlockSpec(memory_space=pl.ANY)
    smem = pl.BlockSpec(memory_space=pltpu.SMEM)
    dma = pltpu.SemaphoreType.DMA
    out, gin, gw = pl.pallas_call(
        kernel,
        out_shape=(
            jax.ShapeDtypeStruct((OWN, D), BF16),
            jax.ShapeDtypeStruct((OWN, D), BF16),
            jax.ShapeDtypeStruct((16, D), F32),
        ),
        in_specs=[vmem, vmem, hbm, hbm, smem],
        out_specs=(vmem, vmem, vmem),
        scratch_shapes=[
            pltpu.VMEM((24, 16, D), BF16),
            pltpu.VMEM((8, 16, D), BF16),
            pltpu.VMEM((8, 16, D), BF16),
            pltpu.VMEM((3 * D, D), BF16),
            pltpu.VMEM((D, D), BF16),
            pltpu.VMEM((EXT, D), BF16),
            pltpu.VMEM((3 * D, EXT), F32),
            pltpu.VMEM((HEADS, HEAD_DIM, OWN), BF16),
            pltpu.VMEM((HEADS, HEAD_DIM, EXT), BF16),
            pltpu.VMEM((HEADS, HEAD_DIM, EXT), BF16),
            pltpu.VMEM((HEADS, HEAD_DIM, OWN), F32),
            pltpu.VMEM((HEADS, HEAD_DIM, EXT), F32),
            pltpu.VMEM((HEADS, 1, OWN), F32),
            pltpu.VMEM((HEADS, 1, EXT), F32),
            pltpu.VMEM((HEADS, HEAD_DIM, OWN), BF16),
            pltpu.VMEM((HEADS, HEAD_DIM, OWN), BF16),
            pltpu.VMEM((HEADS, HEAD_DIM, OWN), BF16),
            pltpu.VMEM((HEADS, HEAD_DIM, EXT), BF16),
            pltpu.VMEM((HEADS, HEAD_DIM, EXT), BF16),
            pltpu.VMEM((OWN, D), BF16),
            pltpu.VMEM((HEADS, HEAD_DIM, OWN), BF16),
            pltpu.VMEM((EXT, OWN), F32),
            pltpu.VMEM((4, 2, 128, D), BF16),
            pltpu.VMEM((4, 2, 128, D), BF16),
            pltpu.VMEM((4, 2, 128, D), F32),
            pltpu.VMEM((CHIPS, 16, D), BF16),
            pltpu.VMEM((CHIPS, 16, D), BF16),
            pltpu.VMEM((16, 16, D), BF16),
            pltpu.VMEM((16, 16, D), BF16),
            pltpu.VMEM((8, 16, D), BF16),
            pltpu.VMEM((8, 16, D), BF16),
            dma((2,)),
            dma((8,)), dma((8,)),
            dma((1,)), dma((1,)),
            dma((4,)), dma((4,)),
            dma((1,)), dma((1,)),
            dma((8,)), dma((8,)),
            dma((1,)), dma((1,)),
        ],
        compiler_params=pltpu.CompilerParams(
            collective_id=0, has_side_effects=True, vmem_limit_bytes=40 * 2**20
        ),
    )(xs, cotangent.reshape(OWN, D), w_qkv, w_out, logit_scale)
    return out.reshape(2, 2, 32, D), gin.reshape(2, 16, 4, D), gw


def solution(mesh):
    return jax.shard_map(
        on_device,
        mesh=mesh,
        in_specs=(P("gx", None, "gy", None), P("gx", "gy", None, None), P(), P(), P()),
        out_specs=(P("gx", "gy", None, None), P("gx", None, "gy", None), P(("gx", "gy"), None)),
        check_vma=False,
    )
```

time: 1380 us -> 54.1 us (0.04); the launches traced: 1360 us -> 53.4 us
  waiting for transfers between devices: 661 us -> 0 us
  local copies, waits for them, and re-layouts: 416 us -> 6.89 us
  other arithmetic: 230 us -> 0 us
  Pallas kernels: 0 us -> 45.9 us
  starting transfers between devices: 29.6 us -> 0 us
  between operations: 16.9 us -> 0.65 us
    reduce_scatter x1 -> x0, waiting for transfers between devices: 634 us -> none  [on_device(): lax.psum_scatter(jnp.concatenate([grad_first, grad_second], axis=0), ('gx...]
    mul x172 -> x0, local copies, waits for them, and re-layouts: 289 us -> none  [the longest x137 233 us: compute(): return (weights[..., None] * head_split(window)).reshape(extent + (D,))]
    reduce_sum x61 -> x0, other arithmetic: 105 us -> none  [the longest x27 50 us: compute(): return (weights[..., None] * head_split(window)).reshape(extent + (D,))]
    broadcast_in_dim x58 -> x0, local copies, waits for them, and re-layouts: 105 us -> none  [the longest x54 98.3 us: compute(): return jnp.sum(head_split(queries) * head_split(window), axis=-1)]
    mul x58 -> x0, other arithmetic: 59.6 us -> none  [the longest x27 51.9 us: compute(): return (weights[..., None] * head_split(window)).reshape(extent + (D,))]
    pallas_call x0 -> x1, Pallas kernels: none -> 45.9 us  [on_device(): pl.pallas_call(kernel, out_shape=(jax.ShapeDtypeStruct((OWN, D), BF16), j...]
    unnamed x26 -> x0, other arithmetic: 21.3 us -> none
    ppermute x8 -> x0, waiting for transfers between devices: 19.1 us -> none  [the longest x4 17.7 us: extended(): lax.ppermute(lax.slice_in_dim(block, 0, width, axis=dim), axis, backward)]
  transfers between devices with their start and end apart: 11 -> 0, of which waited for: 7 -> 0; matrix products, arithmetic and copies ran while one was open for 2% -> 0% of each run, Pallas kernels for 0% -> 0%
where the time goes in v1:
time: 54.1 us; the launch traced here: 53.4 us
  Pallas kernels  45.9 us (85%)
  local copies, waits for them, and re-layouts  6.89 us (13%)
  between operations  0.65 us (1%)
    pallas_call x1, Pallas kernels, on_device(): pl.pallas_call(kernel, out_shape=(jax.ShapeDtypeStruct((OWN, D), BF16), j...  45.9 us
    unnamed x11, local copies, waits for them, and re-layouts  6.2 us

profile of v1, /device:TPU:0, one launch (start us, length us, event | category | flops | bytes accessed | tf_op | source)
XLA Modules:
  0.0 53.4 jit_solution(14098788110452145559)
XLA Ops:
  0.6 0.9 %copy.10 = bf16[2,16,4,512]{3,1,2,0:T(8,128)(2,1)S(1)} copy(bf16[2,16,4,512]{3,2,1,0:T(4,128)(2,1)} %param.5) | data formatting | bytes 262144 | tf_op args[0]
  1.6 0.0 copy-start
  1.6 1.4 %copy-done = bf16[1536,512]{1,0:T(8,128)(2,1)S(1)} copy-done((bf16[1536,512]{1,0:T(8,128)(2,1)S(1)}, bf16[1536,512]{1,0:T(8,128)(2,1)}, u32[]{:S(2)}) %copy-start) | copy-done | bytes 1572888
  3.0 0.0 copy-start.1
  3.0 1.0 %copy-done.1 = bf16[512,512]{1,0:T(8,128)(2,1)S(1)} copy-done((bf16[512,512]{1,0:T(8,128)(2,1)S(1)}, bf16[512,512]{1,0:T(8,128)(2,1)}, u32[]{:S(2)}) %copy-start.1) | copy-done | bytes 524312
  4.0 0.0 copy-start.2
  4.0 0.9 %copy-done.2 = bf16[2,2,32,512]{3,2,1,0:T(8,128)(2,1)S(1)} copy-done((bf16[2,2,32,512]{3,2,1,0:T(8,128)(2,1)S(1)}, bf16[2,2,32,512]{3,2,1,0:T(8,128)(2,1)}, u32[]{:S(2)}) %copy-start.2) | copy-done | bytes 131096
  4.9 0.0 copy-start.3
  4.9 0.7 %copy-done.3 = f32[8]{0:T(128)S(1)} copy-done((f32[8]{0:T(128)S(1)}, f32[8]{0:T(128)}, u32[]{:S(2)}) %copy-start.3) | copy-done | bytes 56
  5.6 45.9 %shard_map.76 = (bf16[128,512]{1,0:T(8,128)(2,1)S(1)}, bf16[128,512]{1,0:T(8,128)(2,1)S(1)}, f32[16,512]{1,0:T(8,128)S(1)}) custom-call(bf16[2,4,16,512]{3,2,1,0:T(8,128)(2,1)S(1)} %bitcast.5, bf16[128,512]{1,0:T(8,128)(2,1)S(1)} %bitcast.6, bf16[1536,512]{1,0:T(8,128)(2,1)S(1)} %copy-done, bf16[512,512]{1,0:T(8,128)(2,1)S(1)} %copy-done.1, f32[8]{0:T(128)S(1)} %copy-done.3), custom_call_target="tpu_custom_call" | custom-call | tf_op jit(solution)/shard_map/pallas_call | solution.py:447
  51.5 0.7 %reshape.17 = bf16[2,16,4,512]{3,2,1,0:T(4,128)(2,1)} reshape(bf16[128,512]{1,0:T(8,128)(2,1)S(1)} %get-tuple-element.7) | data formatting | bytes 262144 | tf_op jit(solution)/shard_map/reshape | solution.py:500
  52.2 0.7 %copy.13 = bf16[2,2,32,512]{3,2,1,0:T(8,128)(2,1)} copy(bf16[2,2,32,512]{3,2,1,0:T(8,128)(2,1)S(1)} %bitcast.7) | data formatting | bytes 262144
  52.8 0.6 %copy.14 = f32[16,512]{1,0:T(8,128)} copy(f32[16,512]{1,0:T(8,128)S(1)} %get-tuple-element.14) | data formatting | bytes 65536
Async XLA Ops:
  1.6 1.4 %copy-start = (bf16[1536,512]{1,0:T(8,128)(2,1)S(1)}, bf16[1536,512]{1,0:T(8,128)(2,1)}, u32[]{:S(2)}) copy-start(bf16[1536,512]{1,0:T(8,128)(2,1)} %wqkv_hbm.1) | copy-start | bytes 4718596
  3.0 1.0 %copy-start.1 = (bf16[512,512]{1,0:T(8,128)(2,1)S(1)}, bf16[512,512]{1,0:T(8,128)(2,1)}, u32[]{:S(2)}) copy-start(bf16[512,512]{1,0:T(8,128)(2,1)} %wout_hbm.1) | copy-start | bytes 1572868
  4.0 0.9 %copy-start.2 = (bf16[2,2,32,512]{3,2,1,0:T(8,128)(2,1)S(1)}, bf16[2,2,32,512]{3,2,1,0:T(8,128)(2,1)}, u32[]{:S(2)}) copy-start(bf16[2,2,32,512]{3,2,1,0:T(8,128)(2,1)} %param.6) | copy-start | bytes 393220
  4.9 0.7 %copy-start.3 = (f32[8]{0:T(128)S(1)}, f32[8]{0:T(128)}, u32[]{:S(2)}) copy-start(f32[8]{0:T(128)} %scale.1) | copy-start | bytes 100

commit v2 on v1

v2 whole, which is shorter than its diff:
```python
import functools

import jax
import jax.numpy as jnp
from jax import lax
from jax.experimental import pallas as pl
from jax.experimental.pallas import tpu as pltpu
from jax.sharding import PartitionSpec as P

MESH = pl.DeviceIdType.MESH
F32 = jnp.float32
BF16 = jnp.bfloat16

D = 512
HEADS = 8
HEAD_DIM = 64
NX, NY, NZ = 32, 16, 32
GX, GY = 16, 8
OWN = 128
EXT = 384
EPSILON = 1e-06
NEGATIVE = -1e30
FACTOR = 1.0 / 128.0

SIDES = ((-1, 0), (1, 0), (0, -1), (0, 1), (-1, -1), (-1, 1), (1, -1), (1, 1))
REGION = {
    (-1, 0): (8, 4),
    (1, 0): (12, 4),
    (0, -1): (16, 2),
    (0, 1): (18, 2),
    (-1, -1): (20, 1),
    (-1, 1): (21, 1),
    (1, -1): (22, 1),
    (1, 1): (23, 1),
}


def dot_nn(a, b):
    return jnp.dot(a, b, preferred_element_type=F32)


def dot_nt(a, b):
    return lax.dot_general(a, b, (((1,), (1,)), ((), ())), preferred_element_type=F32)


def dot_tn(a, b):
    return lax.dot_general(a, b, (((0,), (0,)), ((), ())), preferred_element_type=F32)


def iota(shape, dim):
    return lax.broadcasted_iota(jnp.int32, shape, dim)


def natural_row(r):
    return ((r >> 3) & 1) * 64 + (r & 1) * 32 + (r >> 4) * 4 + ((r >> 1) & 3)


def token_row(r):
    return ((r >> 3) & 1) * 64 + ((r >> 1) & 3) * 16 + (r >> 4) * 2 + (r & 1)


def slab_row(t):
    return ((t >> 6) & 1) * 64 + (t & 15) * 4 + ((t >> 4) & 3)


def gather_rows(index):
    shape = (OWN, OWN)
    return jnp.where(index(iota(shape, 0)) == iota(shape, 1), 1.0, 0.0).astype(BF16)


def scatter_rows(index):
    shape = (OWN, OWN)
    return jnp.where(index(iota(shape, 1)) == iota(shape, 0), 1.0, 0.0).astype(BF16)


def moved(matrix, rows):
    return dot_nn(matrix, rows).astype(BF16)


SLOT_X = {(0, 0): 0, (0, 3): 1, (1, 0): 2, (1, 3): 3, (2, 0): 4, (3, 0): 5}
SLOT_Z = {(0, 2): 0, (1, 2): 1, (2, 2): 2, (2, 3): 3, (3, 2): 4, (3, 3): 5}
SPAN_X = ((0, 2), (2, 2), (4, 1), (5, 1))
SPAN_Z = ((0, 1), (1, 1), (2, 2), (4, 2))


def kernel(
    xs_hbm, cot_hbm, wqkv_hbm, wout_hbm, scale_hbm,
    out, gin, gw,
    xs, cot, scale, xext, cot_send, cot_stage, wqkv, wout, normed, raw,
    q_bd, k_b, v_b, k_t, v_t, q_hat, k_hat, q_inv, k_inv, u_bd, att,
    weights_f, weights_b, gq, gk, gv, cot_tok, cot_t, bias,
    pair_send, pair_recv, sx, sy, sz, rx, ry, rz, tx, ty, tz, fx, fy, fz,
    gn_send, gn_recv, out_send, out_stage,
    w_sem, x_ssem, x_rsem, c_ssem, c_rsem, p_ssem, p_rsem,
    a_ssem, a_rsem, b_ssem, b_rsem, g_ssem, g_rsem, o_ssem, o_rsem,
):
    gx, gy = lax.axis_index("gx"), lax.axis_index("gy")
    core = gx & 1
    at_y = gx >> 2
    at_x = ((gx >> 1) & 1) * 2 + (gy & 1)
    at_z = gy >> 1

    def device_at(y, x, z):
        return (y * 4 + (x >> 1) * 2 + core, z * 2 + (x & 1))

    def exists(side):
        ok = None
        for at, step, size in ((gx, side[0], GX), (gy, side[1], GY)):
            if step:
                here = at > 0 if step < 0 else at < size - 1
                ok = here if ok is None else ok & here
        return ok

    def remote(src, dst, ssem, rsem, to):
        return pltpu.make_async_remote_copy(
            src_ref=src, dst_ref=dst, send_sem=ssem, recv_sem=rsem,
            device_id=to, device_id_type=MESH,
        )

    def wait_for(ref, sem):
        pltpu.make_async_copy(ref, ref, sem).wait()

    load_cot = pltpu.make_async_copy(cot_hbm, cot, w_sem.at[0])
    load_xs = pltpu.make_async_copy(xs_hbm, xs, w_sem.at[1])
    load_scale = pltpu.make_async_copy(scale_hbm, scale, w_sem.at[2])
    load_qkv = pltpu.make_async_copy(wqkv_hbm, wqkv, w_sem.at[3])
    load_out = pltpu.make_async_copy(wout_hbm, wout, w_sem.at[4])
    load_xs.start()
    load_cot.start()
    load_scale.start()
    load_qkv.start()
    load_out.start()

    barrier = pltpu.get_barrier_semaphore()

    def greet(to):
        pl.semaphore_signal(barrier, inc=1, device_id=to, device_id_type=MESH)

    for side in SIDES:
        if side[0]:
            @pl.when(exists(side))
            def _():
                greet((gx + side[0], gy + side[1]))

    def greet_plane(k, carry):
        x, z = (at_x + (k >> 2)) & 3, (at_z + k) & 3
        greet(device_at(at_y, x, z))
        return carry

    def greet_lines(k, carry):
        y = (at_y + 1 + (k >> 2)) & 3
        greet(device_at(y, at_x, (at_z + k) & 3))

        @pl.when((k & 3) > 0)
        def _():
            greet(device_at(y, (at_x + k) & 3, at_z))

        return carry

    lax.fori_loop(1, 16, greet_plane, 0)
    lax.fori_loop(0, 12, greet_lines, 0)

    load_cot.wait()
    cot_send[...] = moved(gather_rows(natural_row), cot[...]).reshape(8, 16, D)
    load_xs.wait()
    load_scale.wait()
    one = jnp.int32(1)
    zero = jnp.int32(0)
    count_x = jnp.where(gx > 0, one, zero) + jnp.where(gx < GX - 1, one, zero)
    count_y = one + jnp.where(gy > 0, one, zero) + jnp.where(gy < GY - 1, one, zero)
    pl.semaphore_wait(barrier, 36 + count_x * count_y)

    def border(ref, side):
        x = {-1: 0, 1: 1}.get(side[0])
        z = {-1: 0, 1: 3}.get(side[1])
        if z is None:
            return ref.at[x]
        if x is None:
            return ref.at[:, z]
        return ref.at[pl.ds(x, 1), z]

    def halo_copy(index, side):
        start, size = REGION[(-side[0], -side[1])]
        return remote(
            border(xs, side), xext.at[pl.ds(start, size)],
            x_ssem.at[index], x_rsem.at[index], (gx + side[0], gy + side[1]),
        )

    for index, side in enumerate(SIDES):
        @pl.when(exists(side))
        def _():
            halo_copy(index, side).start()

    def cot_copy(k, carry):
        to = (gy + k) & (GY - 1)
        remote(
            cot_send.at[to], cot_stage.at[gy], c_ssem.at[0], c_rsem.at[0], (gx, to)
        ).start()
        return carry

    lax.fori_loop(1, GY, cot_copy, 0)
    cot_stage[gy] = cot_send[gy]

    for side in SIDES:
        start, size = REGION[side]

        @pl.when(jnp.logical_not(exists(side)))
        def _():
            xext[pl.ds(start, size)] = jnp.zeros((size, 16, D), BF16)
            gn_recv[pl.ds(start - 8, size)] = jnp.zeros((size, 16, D), BF16)

    def rows_normed(rows):
        return rows * lax.rsqrt(jnp.mean(rows * rows, axis=-1, keepdims=True) + EPSILON)

    x_rows = xs[...].reshape(OWN, D)
    normed[0:OWN] = rows_normed(x_rows.astype(F32)).astype(BF16)
    load_qkv.wait()
    raw[:, 0:OWN] = dot_nt(wqkv[...], normed[0:OWN])

    def pair_rows(base, j):
        return pl.ds(pl.multiple_of(base + j * 128, 128), 128)

    def heads_of(values):
        return values.reshape(2, HEAD_DIM, values.shape[1])

    def head_inverse(values):
        return lax.rsqrt(jnp.mean(values * values, axis=1, keepdims=True) + EPSILON)

    q_bd[...] = jnp.zeros_like(q_bd)
    u_bd[...] = jnp.zeros_like(u_bd)

    def keys_values(j, low, high):
        k = heads_of(raw[pair_rows(D, j), low:high])
        inverse = head_inverse(k)
        hat = (k * inverse).reshape(128, high - low)
        k_hat[j, :, low:high] = hat
        k_inv[j, :, :, low:high] = inverse
        hat_b = hat.astype(BF16)
        k_b[j, :, low:high] = hat_b
        k_t[j, low:high] = hat_b.T
        v = raw[pair_rows(2 * D, j), low:high].astype(BF16)
        v_b[j, :, low:high] = v
        v_t[j, low:high] = v.T

    def own_pairs(j, carry):
        q = heads_of(raw[pair_rows(0, j), 0:OWN])
        inverse = head_inverse(q)
        hat = q * inverse
        q_hat[j] = hat.reshape(128, OWN)
        q_inv[j] = inverse
        for s in range(2):
            q_bd[j, 64 * s : 64 * s + 64, 128 * s : 128 * s + 128] = (
                hat[s] * (scale[2 * j + s] / HEAD_DIM)
            ).astype(BF16)
        keys_values(j, 0, OWN)
        return carry

    lax.fori_loop(0, 4, own_pairs, 0)

    col = iota((16, OWN), 1)
    row_y = iota((16, OWN), 0)
    col_x, col_z = col >> 6, (col >> 4) & 3
    near_y = jnp.abs(row_y - (col & 15)) <= 1

    def bias_cell(cell, carry):
        x = jnp.where(
            cell < 8,
            cell >> 2,
            jnp.where(
                cell < 16,
                jnp.where(cell < 12, -1, 2),
                jnp.where(cell < 20, cell & 1, jnp.where(cell < 22, -1, 2)),
            ),
        )
        z = jnp.where(
            cell < 16,
            cell & 3,
            jnp.where(
                cell < 20, jnp.where(cell < 18, -1, 4), jnp.where((cell & 1) == 0, -1, 4)
            ),
        )
        full_x, full_z = x + 2 * gx, z + 4 * gy
        inside = (full_x >= 0) & (full_x < NX) & (full_z >= 0) & (full_z < NZ)
        x_off = jnp.where(inside, x, jnp.int32(100))
        near = near_y & (jnp.abs(x_off - col_x) <= 1) & (jnp.abs(z - col_z) <= 1)
        block = jnp.where(near, 0.0, NEGATIVE)
        rows = pl.ds(pl.multiple_of(cell * 16, 16), 16)
        bias[rows, 0:OWN] = block
        bias[rows, OWN : 2 * OWN] = block
        return carry

    lax.fori_loop(0, 24, bias_cell, 0)

    load_out.wait()
    wait_for(cot_stage.at[pl.ds(0, GY - 1)], c_rsem.at[0])
    tokens = moved(scatter_rows(token_row), cot_stage[...].reshape(OWN, D))
    cot_tok[...] = tokens
    cot_t[...] = tokens.T.reshape(4, 128, OWN)
    upstream = dot_nn(tokens, wout[...]).astype(BF16).T
    for j in range(4):
        for s in range(2):
            u_bd[j, 64 * s : 64 * s + 64, 128 * s : 128 * s + 128] = upstream[
                128 * j + 64 * s : 128 * j + 64 * s + 64
            ]

    for index, side in enumerate(SIDES):
        opposite = SIDES.index((-side[0], -side[1]))
        start, size = REGION[side]

        @pl.when(exists(side))
        def _():
            wait_for(xext.at[pl.ds(start, size)], x_rsem.at[opposite])

    halo_rows = xext[8:24].reshape(EXT - OWN, D)
    normed[OWN:EXT] = rows_normed(halo_rows.astype(F32)).astype(BF16)
    raw[D : 3 * D, OWN:EXT] = dot_nt(wqkv[D : 3 * D], normed[OWN:EXT])

    def halo_pairs(j, carry):
        keys_values(j, OWN, EXT)
        return carry

    lax.fori_loop(0, 4, halo_pairs, 0)

    def forward(j):
        scores = dot_nn(k_t[j], q_bd[j]) + bias[...]
        shifted = jnp.exp(scores - jnp.max(scores, axis=0, keepdims=True))
        weights = shifted * (1.0 / jnp.sum(shifted, axis=0, keepdims=True))
        weights_f[j] = weights
        rounded = weights.astype(BF16)
        weights_b[j] = rounded
        for s in range(2):
            rows, cols = slice(64 * s, 64 * s + 64), slice(128 * s, 128 * s + 128)
            att[j, rows] = dot_nn(v_b[j, rows], rounded[:, cols]).astype(BF16)

    def back_through(grad, hat, inverse):
        return inverse * (grad - hat * jnp.mean(grad * hat, axis=0, keepdims=True))

    def backward(j):
        grad_w = dot_nn(v_t[j], u_bd[j])
        weights = weights_f[j]
        inner = jnp.sum(weights * grad_w, axis=0, keepdims=True)
        grad_s = (weights * (grad_w - inner)).astype(BF16)
        for s in range(2):
            rows, cols = slice(64 * s, 64 * s + 64), slice(128 * s, 128 * s + 128)
            grad_q = dot_nn(k_b[j, rows], grad_s[:, cols])
            gq[j, rows] = (
                back_through(grad_q, q_hat[j, rows], q_inv[j, s])
                * (scale[2 * j + s] / HEAD_DIM)
            ).astype(BF16)
            grad_k = dot_nt(q_bd[j, rows, cols], grad_s[:, cols])
            gk[j, rows] = back_through(grad_k, k_hat[j, rows], k_inv[j, s]).astype(BF16)
            gv[j, rows] = dot_nt(u_bd[j, rows, cols], weights_b[j, :, cols]).astype(BF16)

    def weight_block(part, j):
        if part == 3:
            return dot_nt(cot_t[j], att[...].reshape(D, OWN))
        if part == 0:
            return dot_nn(gq[j], normed[0:OWN])
        return dot_nn((gk if part == 1 else gv)[j], normed[...])

    def pair_copy(part):
        return remote(
            pair_send.at[part], pair_recv.at[part],
            p_ssem.at[part], p_rsem.at[part], (gx + 1 - 2 * core, gy),
        )

    def send_other(part):
        for which in range(2):
            block = weight_block(part, 2 * which + 1 - core)
            pair_send[part, which] = block.astype(BF16)
        pair_copy(part).start()

    def sum_own(part):
        pair_copy(part).wait_recv()
        for which in range(2):
            total = weight_block(part, 2 * which + core) + pair_recv[part, which].astype(F32)
            blocks = total.astype(BF16).reshape(8, 16, D)
            for r in range(8):
                x, z = 2 * which + (r & 1), r >> 1
                for tile in range(4):
                    value = blocks[r, :, 128 * tile : 128 * tile + 128]
                    if tile == 1:
                        sy[part, x, z] = value
                    elif (part, tile) in SLOT_X:
                        sx[x, SLOT_X[part, tile], z] = value
                    else:
                        sz[z, SLOT_Z[part, tile], x] = value

    def send_lines(slots_x, slots_z):
        def step(k, carry):
            x = (at_x + k) & 3
            remote(
                sx.at[x, slots_x], rx.at[at_x, slots_x], a_ssem.at[0], a_rsem.at[0],
                device_at(at_y, x, at_z),
            ).start()
            z = (at_z + k) & 3
            remote(
                sz.at[z, slots_z], rz.at[at_z, slots_z], a_ssem.at[2], a_rsem.at[2],
                device_at(at_y, at_x, z),
            ).start()
            return carry

        lax.fori_loop(1, 4, step, 0)

    def send_y(part):
        @pl.when(at_y != part)
        def _():
            remote(
                sy.at[part], ry.at[at_y], a_ssem.at[1], a_rsem.at[1],
                device_at(part, at_x, at_z),
            ).start()

    for j in range(4):
        forward(j)
    send_other(3)
    for which in range(2):
        backward(2 * which + 1 - core)
    for part in range(3):
        send_other(part)
    sum_own(3)
    send_y(3)
    send_lines(pl.ds(5, 1), pl.ds(4, 2))
    for which in range(2):
        backward(2 * which + core)
    for part in range(3):
        sum_own(part)
        send_y(part)
    send_lines(pl.ds(0, 5), pl.ds(0, 4))

    grad_kv_halo = jnp.concatenate(
        [gk[:, :, OWN:EXT].reshape(D, EXT - OWN), gv[:, :, OWN:EXT].reshape(D, EXT - OWN)],
        axis=0,
    )
    gn_send[...] = (
        dot_tn(grad_kv_halo, wqkv[D : 3 * D]).astype(BF16).reshape(16, 16, D)
    )

    def grad_copy(index, side):
        start, size = REGION[side]
        target, _ = REGION[(-side[0], -side[1])]
        return remote(
            gn_send.at[pl.ds(start - 8, size)], gn_recv.at[pl.ds(target - 8, size)],
            g_ssem.at[index], g_rsem.at[index], (gx + side[0], gy + side[1]),
        )

    for index, side in enumerate(SIDES):
        @pl.when(exists(side))
        def _():
            grad_copy(index, side).start()

    attended = att[...].reshape(D, OWN).T
    out_rows = (x_rows.astype(F32) + dot_nt(attended, wout[...])).astype(BF16)
    out_send[...] = moved(gather_rows(token_row), out_rows).reshape(8, 16, D)

    def out_copy(k, carry):
        to = (gy + k) & (GY - 1)
        remote(
            out_send.at[to], out_stage.at[gy], o_ssem.at[0], o_rsem.at[0], (gx, to)
        ).start()
        return carry

    lax.fori_loop(1, GY, out_copy, 0)
    out_stage[gy] = out_send[gy]

    def line_sum(own, others, me):
        ry_ = own.astype(F32)
        for k in range(1, 4):
            ry_ = ry_ + others[(me + k) & 3].astype(F32)
        return ry_.astype(BF16)

    wait_for(ry.at[pl.ds(0, 3)], a_rsem.at[1])
    ty[...] = line_sum(sy[at_y], ry, at_y)

    def send_ty(k, carry):
        x, z = (at_x + (k >> 2)) & 3, (at_z + k) & 3
        remote(
            ty.at[x, z], fy.at[at_x * 4 + at_z], b_ssem.at[0], b_rsem.at[0],
            device_at(at_y, x, z),
        ).start()
        return carry

    lax.fori_loop(1, 16, send_ty, 0)
    fy[at_x * 4 + at_z] = ty[at_x, at_z]

    wait_for(rx.at[pl.ds(0, 3)], a_rsem.at[0])
    total = line_sum(sx[at_x], rx, at_x)
    for slot in range(6):
        for z in range(4):
            tx[z, slot] = total[slot, z]
    wait_for(rz.at[pl.ds(0, 3)], a_rsem.at[2])
    total = line_sum(sz[at_z], rz, at_z)
    for slot in range(6):
        for x in range(4):
            tz[x, slot] = total[slot, x]

    for y in range(4):
        first_x, n_x = SPAN_X[y]
        first_z, n_z = SPAN_Z[y]

        def send_planes(k):
            z = (at_z + k) & 3
            remote(
                tx.at[z, pl.ds(first_x, n_x)], fx.at[at_y * 4 + at_z, pl.ds(0, n_x)],
                b_ssem.at[0], b_rsem.at[0], device_at(y, at_x, z),
            ).start()
            x = (at_x + k) & 3
            remote(
                tz.at[x, pl.ds(first_z, n_z)], fz.at[at_y * 4 + at_x, pl.ds(0, n_z)],
                b_ssem.at[0], b_rsem.at[0], device_at(y, x, at_z),
            ).start()

        def step(k, carry):
            send_planes(k)
            return carry

        lax.fori_loop(1, 4, step, 0)

        @pl.when(at_y != y)
        def _():
            send_planes(0)

        @pl.when(at_y == y)
        def _():
            fx[at_y * 4 + at_z, 0:n_x] = tx[at_z, first_x : first_x + n_x]
            fz[at_y * 4 + at_x, 0:n_z] = tz[at_x, first_z : first_z + n_z]

    grad_own = jnp.concatenate(
        [
            gq[...].reshape(D, OWN),
            gk[:, :, 0:OWN].reshape(D, OWN),
            gv[:, :, 0:OWN].reshape(D, OWN),
        ],
        axis=0,
    )
    grad_n = dot_tn(grad_own, wqkv[...]).reshape(2, 4, 16, D)
    for index, side in enumerate(SIDES):
        opposite = SIDES.index((-side[0], -side[1]))
        start, size = REGION[side]

        @pl.when(exists(side))
        def _():
            wait_for(gn_recv.at[pl.ds(start - 8, size)], g_rsem.at[opposite])

    def term(side):
        start, size = REGION[side]
        return gn_recv[start - 8 : start - 8 + size].astype(F32)

    planes = []
    for x in range(2):
        side_x = (-1, 1)[x]
        plane = grad_n[x] + term((side_x, 0))
        low = term((0, -1))[x] + term((side_x, -1))[0]
        high = term((0, 1))[x] + term((side_x, 1))[0]
        planes.append(
            jnp.concatenate(
                [plane[0:1] + low[None], plane[1:3], plane[3:4] + high[None]], axis=0
            )
        )
    grad_n = jnp.concatenate(planes, axis=0).reshape(OWN, D)
    x_float = x_rows.astype(F32)
    inverse = lax.rsqrt(jnp.mean(x_float * x_float, axis=-1, keepdims=True) + EPSILON)
    x_hat = x_float * inverse
    grad_x = inverse * (grad_n - x_hat * jnp.mean(grad_n * x_hat, axis=-1, keepdims=True))
    grad_rows = (cot_tok[...].astype(F32) + grad_x).astype(BF16)
    gin[...] = moved(scatter_rows(slab_row), grad_rows)

    wait_for(out_stage.at[pl.ds(0, GY - 1)], o_rsem.at[0])
    out[...] = moved(scatter_rows(natural_row), out_stage[...].reshape(OWN, D))

    wait_for(rx.at[pl.ds(0, 3), pl.ds(0, 5)], b_rsem.at[0])

    def owned(blocks):
        return jnp.sum(blocks.astype(F32), axis=0) * FACTOR

    gw[:, 0:128] = owned(fx[:, 0])
    gw[:, 128:256] = owned(fy[...])
    gw[:, 256:384] = owned(fz[:, 0])

    @pl.when(at_y < 2)
    def _():
        gw[:, 384:512] = owned(fx[:, 1])

    @pl.when(at_y >= 2)
    def _():
        gw[:, 384:512] = owned(fz[:, 1])

    for index, side in enumerate(SIDES):
        @pl.when(exists(side))
        def _():
            halo_copy(index, side).wait_send()
            grad_copy(index, side).wait_send()

    for part in range(4):
        pair_copy(part).wait_send()
    wait_for(cot_send.at[pl.ds(0, GY - 1)], c_ssem.at[0])
    wait_for(out_send.at[pl.ds(0, GY - 1)], o_ssem.at[0])
    wait_for(rx.at[pl.ds(0, 3)], a_ssem.at[0])
    wait_for(ry.at[pl.ds(0, 3)], a_ssem.at[1])
    wait_for(rz.at[pl.ds(0, 3)], a_ssem.at[2])
    wait_for(rx.at[pl.ds(0, 3), pl.ds(0, 5)], b_ssem.at[0])


def on_device(slab_tokens, cotangent, w_qkv, w_out, logit_scale):
    xs = slab_tokens.transpose(0, 2, 1, 3)
    vmem = pl.BlockSpec(memory_space=pltpu.VMEM)
    hbm = pl.BlockSpec(memory_space=pl.ANY)
    dma = pltpu.SemaphoreType.DMA
    out, gin, gw = pl.pallas_call(
        kernel,
        out_shape=(
            jax.ShapeDtypeStruct((OWN, D), BF16),
            jax.ShapeDtypeStruct((OWN, D), BF16),
            jax.ShapeDtypeStruct((16, D), F32),
        ),
        in_specs=[hbm] * 5,
        out_specs=(vmem, vmem, vmem),
        scratch_shapes=[
            pltpu.VMEM((2, 4, 16, D), BF16),
            pltpu.VMEM((OWN, D), BF16),
            pltpu.SMEM((HEADS,), F32),
            pltpu.VMEM((24, 16, D), BF16),
            pltpu.VMEM((8, 16, D), BF16),
            pltpu.VMEM((8, 16, D), BF16),
            pltpu.VMEM((3 * D, D), BF16),
            pltpu.VMEM((D, D), BF16),
            pltpu.VMEM((EXT, D), BF16),
            pltpu.VMEM((3 * D, EXT), F32),
            pltpu.VMEM((4, 128, 2 * OWN), BF16),
            pltpu.VMEM((4, 128, EXT), BF16),
            pltpu.VMEM((4, 128, EXT), BF16),
            pltpu.VMEM((4, EXT, 128), BF16),
            pltpu.VMEM((4, EXT, 128), BF16),
            pltpu.VMEM((4, 128, OWN), F32),
            pltpu.VMEM((4, 128, EXT), F32),
            pltpu.VMEM((4, 2, 1, OWN), F32),
            pltpu.VMEM((4, 2, 1, EXT), F32),
            pltpu.VMEM((4, 128, 2 * OWN), BF16),
            pltpu.VMEM((4, 128, OWN), BF16),
            pltpu.VMEM((4, EXT, 2 * OWN), F32),
            pltpu.VMEM((4, EXT, 2 * OWN), BF16),
            pltpu.VMEM((4, 128, OWN), BF16),
            pltpu.VMEM((4, 128, EXT), BF16),
            pltpu.VMEM((4, 128, EXT), BF16),
            pltpu.VMEM((OWN, D), BF16),
            pltpu.VMEM((4, 128, OWN), BF16),
            pltpu.VMEM((EXT, 2 * OWN), F32),
            pltpu.VMEM((4, 2, 128, D), BF16),
            pltpu.VMEM((4, 2, 128, D), BF16),
            pltpu.VMEM((4, 6, 4, 16, 128), BF16),
            pltpu.VMEM((4, 4, 4, 16, 128), BF16),
            pltpu.VMEM((4, 6, 4, 16, 128), BF16),
            pltpu.VMEM((4, 6, 4, 16, 128), BF16),
            pltpu.VMEM((4, 4, 4, 16, 128), BF16),
            pltpu.VMEM((4, 6, 4, 16, 128), BF16),
            pltpu.VMEM((4, 6, 16, 128), BF16),
            pltpu.VMEM((4, 4, 16, 128), BF16),
            pltpu.VMEM((4, 6, 16, 128), BF16),
            pltpu.VMEM((16, 2, 16, 128), BF16),
            pltpu.VMEM((16, 16, 128), BF16),
            pltpu.VMEM((16, 2, 16, 128), BF16),
            pltpu.VMEM((16, 16, D), BF16),
            pltpu.VMEM((16, 16, D), BF16),
            pltpu.VMEM((8, 16, D), BF16),
            pltpu.VMEM((8, 16, D), BF16),
            dma((5,)),
            dma((8,)), dma((8,)),
            dma((1,)), dma((1,)),
            dma((4,)), dma((4,)),
            dma((3,)), dma((3,)),
            dma((1,)), dma((1,)),
            dma((8,)), dma((8,)),
            dma((1,)), dma((1,)),
        ],
        compiler_params=pltpu.CompilerParams(
            collective_id=0, has_side_effects=True, vmem_limit_bytes=60 * 2**20
        ),
    )(xs, cotangent.reshape(OWN, D), w_qkv, w_out, logit_scale)
    return out.reshape(2, 2, 32, D), gin.reshape(2, 16, 4, D), gw


def solution(mesh):
    return jax.shard_map(
        on_device,
        mesh=mesh,
        in_specs=(P("gx", None, "gy", None), P("gx", "gy", None, None), P(), P(), P()),
        out_specs=(P("gx", "gy", None, None), P("gx", None, "gy", None), P(("gx", "gy"), None)),
        check_vma=False,
    )
```

time: 54.1 us -> 45 us (0.83)
  Pallas kernels: 45.9 us -> 38 us
  local copies, waits for them, and re-layouts: 6.89 us -> 6.12 us
    pallas_call x1, Pallas kernels: 45.9 us -> 38 us  [on_device(): pl.pallas_call(kernel, out_shape=(jax.ShapeDtypeStruct((OWN, D), BF16), j...]
    unnamed x11 -> x3, local copies, waits for them, and re-layouts: 6.2 us -> 4.52 us
    reshape x1, local copies, waits for them, and re-layouts: 0.69 us -> 1.6 us  [on_device(): return (out.reshape(2, 2, 32, D), gin.reshape(2, 16, 4, D), gw)]
where the time goes in v2:
time: 45 us; the launch traced here: 44.7 us
  Pallas kernels  38 us (84%)
  local copies, waits for them, and re-layouts  6.12 us (14%)
  between operations  0.64 us (1%)
    pallas_call x1, Pallas kernels, on_device(): pl.pallas_call(kernel, out_shape=(jax.ShapeDtypeStruct((OWN, D), BF16), j...  38 us
    unnamed x3, local copies, waits for them, and re-layouts  4.52 us
    reshape x1, local copies, waits for them, and re-layouts, on_device(): return (out.reshape(2, 2, 32, D), gin.reshape(2, 16, 4, D), gw)  1.6 us

profile of v2, /device:TPU:0, one launch (start us, length us, event | category | flops | bytes accessed | tf_op | source)
XLA Modules:
  0.0 44.7 jit_solution(3833775897295922657)
XLA Ops:
  0.6 1.6 %copy.10 = bf16[2,16,4,512]{3,1,2,0:T(8,128)(2,1)} copy(bf16[2,16,4,512]{3,2,1,0:T(4,128)(2,1)} %param.5) | data formatting | bytes 262144 | tf_op args[0]
  2.2 38.0 %shard_map.76 = (bf16[128,512]{1,0:T(8,128)(2,1)}, bf16[128,512]{1,0:T(8,128)(2,1)}, f32[16,512]{1,0:T(8,128)}) custom-call(bf16[2,4,16,512]{3,2,1,0:T(8,128)(2,1)} %bitcast.5, bf16[128,512]{1,0:T(8,128)(2,1)} %bitcast.6, bf16[1536,512]{1,0:T(8,128)(2,1)} %wqkv_hbm.1, bf16[512,512]{1,0:T(8,128)(2,1)} %wout_hbm.1, f32[8]{0:T(128)} %scale_hbm.1), custom_call_target="tpu_custom_call" | custom-call | tf_op jit(solution)/shard_map/pallas_call | solution.py:608
  40.2 1.6 %reshape.17 = bf16[2,16,4,512]{3,2,1,0:T(4,128)(2,1)} reshape(bf16[128,512]{1,0:T(8,128)(2,1)} %get-tuple-element.7) | data formatting | bytes 262144 | tf_op jit(solution)/shard_map/reshape | solution.py:678
  41.8 1.6 %copy.13 = bf16[2,2,32,512]{3,2,1,0:T(8,128)(2,1)} copy(bf16[2,2,32,512]{3,2,1,0:T(8,128)(2,1)} %bitcast.7) | data formatting | bytes 262144
  43.3 1.4 %copy.14 = f32[16,512]{1,0:T(8,128)} copy(f32[16,512]{1,0:T(8,128)} %get-tuple-element.14) | data formatting | bytes 65536

commit v3 on v2

--- a/solution.py
+++ b/solution.py
@@ -77,16 +77,15 @@
     return dot_nn(matrix, rows).astype(BF16)
 
 
-SLOT_X = {(0, 0): 0, (0, 3): 1, (1, 0): 2, (1, 3): 3, (2, 0): 4, (3, 0): 5}
+SLOT_X = {(0, 3): 0, (1, 3): 1}
 SLOT_Z = {(0, 2): 0, (1, 2): 1, (2, 2): 2, (2, 3): 3, (3, 2): 4, (3, 3): 5}
-SPAN_X = ((0, 2), (2, 2), (4, 1), (5, 1))
 SPAN_Z = ((0, 1), (1, 1), (2, 2), (4, 2))
 
 
 def kernel(
-    xs_hbm, cot_hbm, wqkv_hbm, wout_hbm, scale_hbm,
+    slab_hbm, cot_hbm, wqkv_hbm, wout_hbm, scale_hbm,
     out, gin, gw,
-    xs, cot, scale, xext, cot_send, cot_stage, wqkv, wout, normed, raw,
+    slab, xs, cot, scale, xext, cot_send, cot_stage, wqkv, wout, normed, raw,
     q_bd, k_b, v_b, k_t, v_t, q_hat, k_hat, q_inv, k_inv, u_bd, att,
     weights_f, weights_b, gq, gk, gv, cot_tok, cot_t, bias,
     pair_send, pair_recv, sx, sy, sz, rx, ry, rz, tx, ty, tz, fx, fy, fz,
@@ -121,11 +120,11 @@
         pltpu.make_async_copy(ref, ref, sem).wait()
 
     load_cot = pltpu.make_async_copy(cot_hbm, cot, w_sem.at[0])
-    load_xs = pltpu.make_async_copy(xs_hbm, xs, w_sem.at[1])
+    load_slab = pltpu.make_async_copy(slab_hbm, slab, w_sem.at[1])
     load_scale = pltpu.make_async_copy(scale_hbm, scale, w_sem.at[2])
     load_qkv = pltpu.make_async_copy(wqkv_hbm, wqkv, w_sem.at[3])
     load_out = pltpu.make_async_copy(wout_hbm, wout, w_sem.at[4])
-    load_xs.start()
+    load_slab.start()
     load_cot.start()
     load_scale.start()
     load_qkv.start()
@@ -160,10 +159,9 @@
     lax.fori_loop(1, 16, greet_plane, 0)
     lax.fori_loop(0, 12, greet_lines, 0)
 
-    load_cot.wait()
-    cot_send[...] = moved(gather_rows(natural_row), cot[...]).reshape(8, 16, D)
-    load_xs.wait()
-    load_scale.wait()
+    load_slab.wait()
+    slab_rows = slab[...].astype(F32).reshape(OWN, D).astype(BF16)
+    xs[...] = moved(gather_rows(slab_row), slab_rows).reshape(2, 4, 16, D)
     one = jnp.int32(1)
     zero = jnp.int32(0)
     count_x = jnp.where(gx > 0, one, zero) + jnp.where(gx < GX - 1, one, zero)
@@ -191,15 +189,16 @@
         def _():
             halo_copy(index, side).start()
 
+    load_cot.wait()
+    cot_send[...] = moved(gather_rows(natural_row), cot[...]).reshape(8, 16, D)
+    load_scale.wait()
+
     def cot_copy(k, carry):
         to = (gy + k) & (GY - 1)
         remote(
             cot_send.at[to], cot_stage.at[gy], c_ssem.at[0], c_rsem.at[0], (gx, to)
         ).start()
         return carry
-
-    lax.fori_loop(1, GY, cot_copy, 0)
-    cot_stage[gy] = cot_send[gy]
 
     for side in SIDES:
         start, size = REGION[side]
@@ -291,18 +290,6 @@
 
     lax.fori_loop(0, 24, bias_cell, 0)
 
-    load_out.wait()
-    wait_for(cot_stage.at[pl.ds(0, GY - 1)], c_rsem.at[0])
-    tokens = moved(scatter_rows(token_row), cot_stage[...].reshape(OWN, D))
-    cot_tok[...] = tokens
-    cot_t[...] = tokens.T.reshape(4, 128, OWN)
-    upstream = dot_nn(tokens, wout[...]).astype(BF16).T
-    for j in range(4):
-        for s in range(2):
-            u_bd[j, 64 * s : 64 * s + 64, 128 * s : 128 * s + 128] = upstream[
-                128 * j + 64 * s : 128 * j + 64 * s + 64
-            ]
-
     for index, side in enumerate(SIDES):
         opposite = SIDES.index((-side[0], -side[1]))
         start, size = REGION[side]
@@ -310,6 +297,9 @@
         @pl.when(exists(side))
         def _():
             wait_for(xext.at[pl.ds(start, size)], x_rsem.at[opposite])
+
+    lax.fori_loop(1, GY, cot_copy, 0)
+    cot_stage[gy] = cot_send[gy]
 
     halo_rows = xext[8:24].reshape(EXT - OWN, D)
     normed[OWN:EXT] = rows_normed(halo_rows.astype(F32)).astype(BF16)
@@ -379,23 +369,25 @@
                 x, z = 2 * which + (r & 1), r >> 1
                 for tile in range(4):
                     value = blocks[r, :, 128 * tile : 128 * tile + 128]
-                    if tile == 1:
-                        sy[part, x, z] = value
+                    if tile < 2:
+                        sy[part, x, z, :, 128 * tile : 128 * tile + 128] = value
                     elif (part, tile) in SLOT_X:
                         sx[x, SLOT_X[part, tile], z] = value
                     else:
                         sz[z, SLOT_Z[part, tile], x] = value
 
-    def send_lines(slots_x, slots_z):
+    def send_x(k, carry):
+        x = (at_x + k) & 3
+        remote(
+            sx.at[x], rx.at[at_x], a_ssem.at[0], a_rsem.at[0], device_at(at_y, x, at_z)
+        ).start()
+        return carry
+
+    def send_z(slots):
         def step(k, carry):
-            x = (at_x + k) & 3
-            remote(
-                sx.at[x, slots_x], rx.at[at_x, slots_x], a_ssem.at[0], a_rsem.at[0],
-                device_at(at_y, x, at_z),
-            ).start()
             z = (at_z + k) & 3
             remote(
-                sz.at[z, slots_z], rz.at[at_z, slots_z], a_ssem.at[2], a_rsem.at[2],
+                sz.at[z, slots], rz.at[at_z, slots], a_ssem.at[2], a_rsem.at[2],
                 device_at(at_y, at_x, z),
             ).start()
             return carry
@@ -412,6 +404,19 @@
 
     for j in range(4):
         forward(j)
+
+    load_out.wait()
+    wait_for(cot_stage.at[pl.ds(0, GY - 1)], c_rsem.at[0])
+    tokens = moved(scatter_rows(token_row), cot_stage[...].reshape(OWN, D))
+    cot_tok[...] = tokens
+    cot_t[...] = tokens.T.reshape(4, 128, OWN)
+    upstream = dot_nn(tokens, wout[...]).astype(BF16).T
+    for j in range(4):
+        for s in range(2):
+            u_bd[j, 64 * s : 64 * s + 64, 128 * s : 128 * s + 128] = upstream[
+                128 * j + 64 * s : 128 * j + 64 * s + 64
+            ]
+
     send_other(3)
     for which in range(2):
         backward(2 * which + 1 - core)
@@ -419,13 +424,14 @@
         send_other(part)
     sum_own(3)
     send_y(3)
-    send_lines(pl.ds(5, 1), pl.ds(4, 2))
+    send_z(pl.ds(4, 2))
     for which in range(2):
         backward(2 * which + core)
     for part in range(3):
         sum_own(part)
         send_y(part)
-    send_lines(pl.ds(0, 5), pl.ds(0, 4))
+    send_z(pl.ds(0, 4))
+    lax.fori_loop(1, 4, send_x, 0)
 
     grad_kv_halo = jnp.concatenate(
         [gk[:, :, OWN:EXT].reshape(D, EXT - OWN), gv[:, :, OWN:EXT].reshape(D, EXT - OWN)],
@@ -468,6 +474,58 @@
             ry_ = ry_ + others[(me + k) & 3].astype(F32)
         return ry_.astype(BF16)
 
+    wait_for(rx.at[pl.ds(0, 3)], a_rsem.at[0])
+    total = line_sum(sx[at_x], rx, at_x)
+    for slot in range(2):
+        for z in range(4):
+            tx[z, slot] = total[slot, z]
+
+    for y in range(2):
+        def send_tx(k, carry):
+            z = (at_z + k) & 3
+            remote(
+                tx.at[z, y], fx.at[at_y * 4 + at_z],
+                b_ssem.at[0], b_rsem.at[0], device_at(y, at_x, z),
+            ).start()
+            return carry
+
+        lax.fori_loop(1, 4, send_tx, 0)
+
+        @pl.when(at_y != y)
+        def _():
+            send_tx(0, 0)
+
+        @pl.when(at_y == y)
+        def _():
+            fx[at_y * 4 + at_z] = tx[at_z, y]
+
+    wait_for(rz.at[pl.ds(0, 3)], a_rsem.at[2])
+    total = line_sum(sz[at_z], rz, at_z)
+    for slot in range(6):
+        for x in range(4):
+            tz[x, slot] = total[slot, x]
+
+    for y in range(4):
+        first, count = SPAN_Z[y]
+
+        def send_tz(k, carry):
+            x = (at_x + k) & 3
+            remote(
+                tz.at[x, pl.ds(first, count)], fz.at[at_y * 4 + at_x, pl.ds(0, count)],
+                b_ssem.at[0], b_rsem.at[0], device_at(y, x, at_z),
+            ).start()
+            return carry
+
+        lax.fori_loop(1, 4, send_tz, 0)
+
+        @pl.when(at_y != y)
+        def _():
+            send_tz(0, 0)
+
+        @pl.when(at_y == y)
+        def _():
+            fz[at_y * 4 + at_x, 0:count] = tz[at_x, first : first + count]
+
     wait_for(ry.at[pl.ds(0, 3)], a_rsem.at[1])
     ty[...] = line_sum(sy[at_y], ry, at_y)
 
@@ -481,48 +539,6 @@
 
     lax.fori_loop(1, 16, send_ty, 0)
     fy[at_x * 4 + at_z] = ty[at_x, at_z]
-
-    wait_for(rx.at[pl.ds(0, 3)], a_rsem.at[0])
-    total = line_sum(sx[at_x], rx, at_x)
-    for slot in range(6):
-        for z in range(4):
-            tx[z, slot] = total[slot, z]
-    wait_for(rz.at[pl.ds(0, 3)], a_rsem.at[2])
-    total = line_sum(sz[at_z], rz, at_z)
-    for slot in range(6):
-        for x in range(4):
-            tz[x, slot] = total[slot, x]
-
-    for y in range(4):
-        first_x, n_x = SPAN_X[y]
-        first_z, n_z = SPAN_Z[y]
-
-        def send_planes(k):
-            z = (at_z + k) & 3
-            remote(
-                tx.at[z, pl.ds(first_x, n_x)], fx.at[at_y * 4 + at_z, pl.ds(0, n_x)],
-                b_ssem.at[0], b_rsem.at[0], device_at(y, at_x, z),
-            ).start()
-            x = (at_x + k) & 3
-            remote(
-                tz.at[x, pl.ds(first_z, n_z)], fz.at[at_y * 4 + at_x, pl.ds(0, n_z)],
-                b_ssem.at[0], b_rsem.at[0], device_at(y, x, at_z),
-            ).start()
-
-        def step(k, carry):
-            send_planes(k)
-            return carry
-
-        lax.fori_loop(1, 4, step, 0)
-
-        @pl.when(at_y != y)
-        def _():
-            send_planes(0)
-
-        @pl.when(at_y == y)
-        def _():
-            fx[at_y * 4 + at_z, 0:n_x] = tx[at_z, first_x : first_x + n_x]
-            fz[at_y * 4 + at_x, 0:n_z] = tz[at_x, first_z : first_z + n_z]
 
     grad_own = jnp.concatenate(
         [
@@ -567,18 +583,17 @@
     wait_for(out_stage.at[pl.ds(0, GY - 1)], o_rsem.at[0])
     out[...] = moved(scatter_rows(natural_row), out_stage[...].reshape(OWN, D))
 
-    wait_for(rx.at[pl.ds(0, 3), pl.ds(0, 5)], b_rsem.at[0])
+    wait_for(rz.at[pl.ds(0, 3), pl.ds(0, 5)], b_rsem.at[0])
 
     def owned(blocks):
         return jnp.sum(blocks.astype(F32), axis=0) * FACTOR
 
-    gw[:, 0:128] = owned(fx[:, 0])
-    gw[:, 128:256] = owned(fy[...])
+    gw[:, 0:256] = owned(fy[...])
     gw[:, 256:384] = owned(fz[:, 0])
 
     @pl.when(at_y < 2)
     def _():
-        gw[:, 384:512] = owned(fx[:, 1])
+        gw[:, 384:512] = owned(fx[...])
 
     @pl.when(at_y >= 2)
     def _():
@@ -597,24 +612,30 @@
     wait_for(rx.at[pl.ds(0, 3)], a_ssem.at[0])
     wait_for(ry.at[pl.ds(0, 3)], a_ssem.at[1])
     wait_for(rz.at[pl.ds(0, 3)], a_ssem.at[2])
-    wait_for(rx.at[pl.ds(0, 3), pl.ds(0, 5)], b_ssem.at[0])
+    wait_for(rz.at[pl.ds(0, 3), pl.ds(0, 5)], b_ssem.at[0])
+
+
+def placed(out, gin, gw, out_at, gin_at, gw_at):
+    out_at[...] = out[...]
+    gin_at[...] = gin[...].astype(F32).reshape(2, 16, 4, D).astype(BF16)
+    gw_at[...] = gw[...]
 
 
 def on_device(slab_tokens, cotangent, w_qkv, w_out, logit_scale):
-    xs = slab_tokens.transpose(0, 2, 1, 3)
     vmem = pl.BlockSpec(memory_space=pltpu.VMEM)
     hbm = pl.BlockSpec(memory_space=pl.ANY)
     dma = pltpu.SemaphoreType.DMA
     out, gin, gw = pl.pallas_call(
         kernel,
         out_shape=(
-            jax.ShapeDtypeStruct((OWN, D), BF16),
-            jax.ShapeDtypeStruct((OWN, D), BF16),
-            jax.ShapeDtypeStruct((16, D), F32),
+            pltpu.VMEM((OWN, D), BF16),
+            pltpu.VMEM((OWN, D), BF16),
+            pltpu.VMEM((16, D), F32),
         ),
         in_specs=[hbm] * 5,
         out_specs=(vmem, vmem, vmem),
         scratch_shapes=[
+            pltpu.VMEM((2, 16, 4, D), BF16),
             pltpu.VMEM((2, 4, 16, D), BF16),
             pltpu.VMEM((OWN, D), BF16),
             pltpu.SMEM((HEADS,), F32),
@@ -646,17 +667,17 @@
             pltpu.VMEM((EXT, 2 * OWN), F32),
             pltpu.VMEM((4, 2, 128, D), BF16),
             pltpu.VMEM((4, 2, 128, D), BF16),
+            pltpu.VMEM((4, 2, 4, 16, 128), BF16),
+            pltpu.VMEM((4, 4, 4, 16, 256), BF16),
             pltpu.VMEM((4, 6, 4, 16, 128), BF16),
-            pltpu.VMEM((4, 4, 4, 16, 128), BF16),
+            pltpu.VMEM((4, 2, 4, 16, 128), BF16),
+            pltpu.VMEM((4, 4, 4, 16, 256), BF16),
             pltpu.VMEM((4, 6, 4, 16, 128), BF16),
-            pltpu.VMEM((4, 6, 4, 16, 128), BF16),
-            pltpu.VMEM((4, 4, 4, 16, 128), BF16),
-            pltpu.VMEM((4, 6, 4, 16, 128), BF16),
+            pltpu.VMEM((4, 2, 16, 128), BF16),
+            pltpu.VMEM((4, 4, 16, 256), BF16),
             pltpu.VMEM((4, 6, 16, 128), BF16),
-            pltpu.VMEM((4, 4, 16, 128), BF16),
-            pltpu.VMEM((4, 6, 16, 128), BF16),
-            pltpu.VMEM((16, 2, 16, 128), BF16),
             pltpu.VMEM((16, 16, 128), BF16),
+            pltpu.VMEM((16, 16, 256), BF16),
             pltpu.VMEM((16, 2, 16, 128), BF16),
             pltpu.VMEM((16, 16, D), BF16),
             pltpu.VMEM((16, 16, D), BF16),
@@ -672,10 +693,21 @@
             dma((1,)), dma((1,)),
         ],
         compiler_params=pltpu.CompilerParams(
-            collective_id=0, has_side_effects=True, vmem_limit_bytes=60 * 2**20
+            collective_id=0, has_side_effects=True, vmem_limit_bytes=57 * 2**20
         ),
-    )(xs, cotangent.reshape(OWN, D), w_qkv, w_out, logit_scale)
-    return out.reshape(2, 2, 32, D), gin.reshape(2, 16, 4, D), gw
+    )(slab_tokens, cotangent.reshape(OWN, D), w_qkv, w_out, logit_scale)
+    out, gin, gw = pl.pallas_call(
+        placed,
+        out_shape=(
+            jax.ShapeDtypeStruct((OWN, D), BF16),
+            jax.ShapeDtypeStruct((2, 16, 4, D), BF16),
+            jax.ShapeDtypeStruct((16, D), F32),
+        ),
+        in_specs=[vmem] * 3,
+        out_specs=(vmem,) * 3,
+        compiler_params=pltpu.CompilerParams(vmem_limit_bytes=8 * 2**20),
+    )(out, gin, gw)
+    return out.reshape(2, 2, 32, D), gin, gw
 
 
 def solution(mesh):

time: 45 us -> 37 us (0.82)
  local copies, waits for them, and re-layouts: 6.12 us -> 0 us
  Pallas kernels: 38 us -> 36.2 us
    unnamed x3 -> x0, local copies, waits for them, and re-layouts: 4.52 us -> none
    pallas_call x1 -> x2, Pallas kernels: 38 us -> 36.2 us  [the longest x1 35.5 us: on_device(): pl.pallas_call(kernel, out_shape=(pltpu.VMEM((OWN, D), BF16), pltpu.VMEM(...]
    reshape x1 -> x0, local copies, waits for them, and re-layouts: 1.6 us -> none  [on_device(): return (out.reshape(2, 2, 32, D), gin.reshape(2, 16, 4, D), gw)]
where the time goes in v3:
time: 37 us; the launch traced here: 36.9 us
  Pallas kernels  36.2 us (98%)
  between operations  0.64 us (2%)
    pallas_call x1, Pallas kernels, on_device(): pl.pallas_call(kernel, out_shape=(pltpu.VMEM((OWN, D), BF16), pltpu.VMEM(...  35.5 us

profile of v3, /device:TPU:0, one launch (start us, length us, event | category | flops | bytes accessed | tf_op | source)
XLA Modules:
  0.0 36.9 jit_solution(4119465454561532728)
XLA Ops:
  0.6 35.5 %shard_map.76 = (bf16[128,512]{1,0:T(8,128)(2,1)S(1)}, bf16[128,512]{1,0:T(8,128)(2,1)S(1)}, f32[16,512]{1,0:T(8,128)S(1)}) custom-call(bf16[2,16,4,512]{3,2,1,0:T(4,128)(2,1)} %slab_hbm.1, bf16[128,512]{1,0:T(8,128)(2,1)} %bitcast.2, bf16[1536,512]{1,0:T(8,128)(2,1)} %wqkv_hbm.1, bf16[512,512]{1,0:T(8,128)(2,1)} %wout_hbm.1, f32[8]{0:T(128)} %scale_hbm.1), custom_call_target="tpu_custom_call" | custom-call | tf_op jit(solution)/shard_map/pallas_call | solution.py:628
  36.1 0.7 %shard_map.77 = (bf16[128,512]{1,0:T(8,128)(2,1)}, bf16[2,16,4,512]{3,2,1,0:T(4,128)(2,1)}, f32[16,512]{1,0:T(8,128)}) custom-call(bf16[128,512]{1,0:T(8,128)(2,1)S(1)} %get-tuple-element.9.out, bf16[128,512]{1,0:T(8,128)(2,1)S(1)} %get-tuple-element.10.gin, f32[16,512]{1,0:T(8,128)S(1)} %get-tuple-element.11.gw), custom_call_target="tpu_custom_call" | custom-call | tf_op jit(solution)/shard_map/pallas_call | solution.py:699

commit v4 on v3

--- a/solution.py
+++ b/solution.py
@@ -77,9 +77,10 @@
     return dot_nn(matrix, rows).astype(BF16)
 
 
-SLOT_X = {(0, 3): 0, (1, 3): 1}
-SLOT_Z = {(0, 2): 0, (1, 2): 1, (2, 2): 2, (2, 3): 3, (3, 2): 4, (3, 3): 5}
-SPAN_Z = ((0, 1), (1, 1), (2, 2), (4, 2))
+SLOT_X = {(0, 1): 0, (0, 3): 1, (1, 1): 2, (2, 1): 3, (3, 0): 4, (3, 1): 5}
+SLOT_Z = {(0, 2): 0, (1, 2): 1, (1, 3): 2, (2, 2): 3, (2, 3): 4, (3, 2): 5, (3, 3): 6}
+SPAN_X = ((0, 2), (2, 1), (3, 1), (4, 2))
+SPAN_Z = ((0, 1), (1, 2), (3, 2), (5, 2))
 
 
 def kernel(
@@ -87,7 +88,7 @@
     out, gin, gw,
     slab, xs, cot, scale, xext, cot_send, cot_stage, wqkv, wout, normed, raw,
     q_bd, k_b, v_b, k_t, v_t, q_hat, k_hat, q_inv, k_inv, u_bd, att,
-    weights_f, weights_b, gq, gk, gv, cot_tok, cot_t, bias,
+    weights_f, weights_b, inverse, grad_f, grad_b, gq, gk, gv, cot_tok, cot_t, bias,
     pair_send, pair_recv, sx, sy, sz, rx, ry, rz, tx, ty, tz, fx, fy, fz,
     gn_send, gn_recv, out_send, out_stage,
     w_sem, x_ssem, x_rsem, c_ssem, c_rsem, p_ssem, p_rsem,
@@ -230,10 +231,10 @@
 
     def keys_values(j, low, high):
         k = heads_of(raw[pair_rows(D, j), low:high])
-        inverse = head_inverse(k)
-        hat = (k * inverse).reshape(128, high - low)
+        rms = head_inverse(k)
+        hat = (k * rms).reshape(128, high - low)
         k_hat[j, :, low:high] = hat
-        k_inv[j, :, :, low:high] = inverse
+        k_inv[j, :, :, low:high] = rms
         hat_b = hat.astype(BF16)
         k_b[j, :, low:high] = hat_b
         k_t[j, low:high] = hat_b.T
@@ -243,10 +244,10 @@
 
     def own_pairs(j, carry):
         q = heads_of(raw[pair_rows(0, j), 0:OWN])
-        inverse = head_inverse(q)
-        hat = q * inverse
+        rms = head_inverse(q)
+        hat = q * rms
         q_hat[j] = hat.reshape(128, OWN)
-        q_inv[j] = inverse
+        q_inv[j] = rms
         for s in range(2):
             q_bd[j, 64 * s : 64 * s + 64, 128 * s : 128 * s + 128] = (
                 hat[s] * (scale[2 * j + s] / HEAD_DIM)
@@ -290,6 +291,9 @@
 
     lax.fori_loop(0, 24, bias_cell, 0)
 
+    lax.fori_loop(1, GY, cot_copy, 0)
+    cot_stage[gy] = cot_send[gy]
+
     for index, side in enumerate(SIDES):
         opposite = SIDES.index((-side[0], -side[1]))
         start, size = REGION[side]
@@ -298,9 +302,6 @@
         def _():
             wait_for(xext.at[pl.ds(start, size)], x_rsem.at[opposite])
 
-    lax.fori_loop(1, GY, cot_copy, 0)
-    cot_stage[gy] = cot_send[gy]
-
     halo_rows = xext[8:24].reshape(EXT - OWN, D)
     normed[OWN:EXT] = rows_normed(halo_rows.astype(F32)).astype(BF16)
     raw[D : 3 * D, OWN:EXT] = dot_nt(wqkv[D : 3 * D], normed[OWN:EXT])
@@ -309,37 +310,83 @@
         keys_values(j, OWN, EXT)
         return carry
 
-    lax.fori_loop(0, 4, halo_pairs, 0)
-
-    def forward(j):
-        scores = dot_nn(k_t[j], q_bd[j]) + bias[...]
-        shifted = jnp.exp(scores - jnp.max(scores, axis=0, keepdims=True))
-        weights = shifted * (1.0 / jnp.sum(shifted, axis=0, keepdims=True))
-        weights_f[j] = weights
-        rounded = weights.astype(BF16)
-        weights_b[j] = rounded
+    lax.fori_loop(0, 4, halo_pairs, 0, unroll=4)
+
+    steps = [slice(low, low + 128) for low in range(0, EXT, 128)]
+    halves = [(slice(64 * s, 64 * s + 64), slice(128 * s, 128 * s + 128)) for s in range(2)]
+
+    def score_step(j, rows, top):
+        scores = dot_nn(k_t[j, rows], q_bd[j]) + bias[rows]
+        weights_f[j, rows] = scores
+        here = jnp.max(scores, axis=0, keepdims=True)
+        return here if top is None else jnp.maximum(top, here)
+
+    def exp_step(j, rows, top, total):
+        shifted = jnp.exp(weights_f[j, rows] - top)
+        weights_f[j, rows] = shifted
+        weights_b[j, rows] = shifted.astype(BF16)
+        here = jnp.sum(shifted, axis=0, keepdims=True)
+        return here if total is None else total + here
+
+    def attend(j, total):
+        scaled = 1.0 / total
+        inverse[j] = scaled
+        for rows, cols in halves:
+            att[j, rows] = (
+                dot_nn(v_b[j, rows], weights_b[j, :, cols]) * scaled[:, cols]
+            ).astype(BF16)
+
+    def forward_pairs():
+        tops = [None] * 5
+        for j in range(5):
+            total = None
+            for rows in steps:
+                if j < 4:
+                    tops[j] = score_step(j, rows, tops[j])
+                if j:
+                    total = exp_step(j - 1, rows, tops[j - 1], total)
+            if j:
+                attend(j - 1, total)
+
+    def back_through(grad, hat, inverse_rms):
+        return inverse_rms * (grad - hat * jnp.mean(grad * hat, axis=0, keepdims=True))
+
+    def grad_weight_step(j, t, rows, inner):
+        grad_w = dot_nn(v_t[j, rows], u_bd[j])
+        grad_f[t, rows] = grad_w
+        here = jnp.sum(weights_f[j, rows] * grad_w, axis=0, keepdims=True)
+        return here if inner is None else inner + here
+
+    def grad_score_step(j, t, rows, inner):
+        scaled = inverse[j]
+        grad_b[t, rows] = (
+            weights_f[j, rows] * ((grad_f[t, rows] - inner * scaled) * scaled)
+        ).astype(BF16)
+
+    def grad_heads(j, t, s):
+        rows, cols = halves[s]
+        grad_q = dot_nn(k_b[j, rows], grad_b[t, :, cols])
+        gq[j, rows] = (
+            back_through(grad_q, q_hat[j, rows], q_inv[j, s]) * (scale[2 * j + s] / HEAD_DIM)
+        ).astype(BF16)
+        grad_k = dot_nt(q_bd[j, rows, cols], grad_b[t, :, cols])
+        gk[j, rows] = back_through(grad_k, k_hat[j, rows], k_inv[j, s]).astype(BF16)
+        up = (u_bd[j, rows, cols].astype(F32) * inverse[j][:, cols]).astype(BF16)
+        gv[j, rows] = dot_nt(up, weights_b[j, :, cols]).astype(BF16)
+
+    def backward_pairs(first, second):
+        inner = [None, None]
+        for rows in steps:
+            inner[0] = grad_weight_step(first, 0, rows, inner[0])
+        for rows in steps:
+            inner[1] = grad_weight_step(second, 1, rows, inner[1])
+            grad_score_step(first, 0, rows, inner[0])
+        grad_heads(first, 0, 0)
+        for rows in steps:
+            grad_score_step(second, 1, rows, inner[1])
+        grad_heads(first, 0, 1)
         for s in range(2):
-            rows, cols = slice(64 * s, 64 * s + 64), slice(128 * s, 128 * s + 128)
-            att[j, rows] = dot_nn(v_b[j, rows], rounded[:, cols]).astype(BF16)
-
-    def back_through(grad, hat, inverse):
-        return inverse * (grad - hat * jnp.mean(grad * hat, axis=0, keepdims=True))
-
-    def backward(j):
-        grad_w = dot_nn(v_t[j], u_bd[j])
-        weights = weights_f[j]
-        inner = jnp.sum(weights * grad_w, axis=0, keepdims=True)
-        grad_s = (weights * (grad_w - inner)).astype(BF16)
-        for s in range(2):
-            rows, cols = slice(64 * s, 64 * s + 64), slice(128 * s, 128 * s + 128)
-            grad_q = dot_nn(k_b[j, rows], grad_s[:, cols])
-            gq[j, rows] = (
-                back_through(grad_q, q_hat[j, rows], q_inv[j, s])
-                * (scale[2 * j + s] / HEAD_DIM)
-            ).astype(BF16)
-            grad_k = dot_nt(q_bd[j, rows, cols], grad_s[:, cols])
-            gk[j, rows] = back_through(grad_k, k_hat[j, rows], k_inv[j, s]).astype(BF16)
-            gv[j, rows] = dot_nt(u_bd[j, rows, cols], weights_b[j, :, cols]).astype(BF16)
+            grad_heads(second, 1, s)
 
     def weight_block(part, j):
         if part == 3:
@@ -369,26 +416,24 @@
                 x, z = 2 * which + (r & 1), r >> 1
                 for tile in range(4):
                     value = blocks[r, :, 128 * tile : 128 * tile + 128]
-                    if tile < 2:
-                        sy[part, x, z, :, 128 * tile : 128 * tile + 128] = value
-                    elif (part, tile) in SLOT_X:
+                    if (part, tile) in SLOT_X:
                         sx[x, SLOT_X[part, tile], z] = value
+                    elif (part, tile) in SLOT_Z:
+                        sz[z, SLOT_Z[part, tile], x] = value
                     else:
-                        sz[z, SLOT_Z[part, tile], x] = value
-
-    def send_x(k, carry):
-        x = (at_x + k) & 3
-        remote(
-            sx.at[x], rx.at[at_x], a_ssem.at[0], a_rsem.at[0], device_at(at_y, x, at_z)
-        ).start()
-        return carry
-
-    def send_z(slots):
+                        sy[part, x, z] = value
+
+    def send_lines(slots_x, slots_z):
         def step(k, carry):
             z = (at_z + k) & 3
             remote(
-                sz.at[z, slots], rz.at[at_z, slots], a_ssem.at[2], a_rsem.at[2],
+                sz.at[z, slots_z], rz.at[at_z, slots_z], a_ssem.at[2], a_rsem.at[2],
                 device_at(at_y, at_x, z),
+            ).start()
+            x = (at_x + k) & 3
+            remote(
+                sx.at[x, slots_x], rx.at[at_x, slots_x], a_ssem.at[0], a_rsem.at[0],
+                device_at(at_y, x, at_z),
             ).start()
             return carry
 
@@ -402,8 +447,7 @@
                 device_at(part, at_x, at_z),
             ).start()
 
-    for j in range(4):
-        forward(j)
+    forward_pairs()
 
     load_out.wait()
     wait_for(cot_stage.at[pl.ds(0, GY - 1)], c_rsem.at[0])
@@ -418,20 +462,30 @@
             ]
 
     send_other(3)
-    for which in range(2):
-        backward(2 * which + 1 - core)
+    attended = att[...].reshape(D, OWN).T
+    out_rows = (x_rows.astype(F32) + dot_nt(attended, wout[...])).astype(BF16)
+    out_send[...] = moved(gather_rows(token_row), out_rows).reshape(8, 16, D)
+
+    def out_copy(k, carry):
+        to = (gy + k) & (GY - 1)
+        remote(
+            out_send.at[to], out_stage.at[gy], o_ssem.at[0], o_rsem.at[0], (gx, to)
+        ).start()
+        return carry
+
+    lax.fori_loop(1, GY, out_copy, 0)
+    out_stage[gy] = out_send[gy]
+
+    backward_pairs(1 - core, 3 - core)
     for part in range(3):
         send_other(part)
     sum_own(3)
-    send_y(3)
-    send_z(pl.ds(4, 2))
-    for which in range(2):
-        backward(2 * which + core)
+    send_lines(pl.ds(4, 2), pl.ds(5, 2))
+    backward_pairs(core, 2 + core)
     for part in range(3):
         sum_own(part)
         send_y(part)
-    send_z(pl.ds(0, 4))
-    lax.fori_loop(1, 4, send_x, 0)
+    send_lines(pl.ds(0, 4), pl.ds(0, 5))
 
     grad_kv_halo = jnp.concatenate(
         [gk[:, :, OWN:EXT].reshape(D, EXT - OWN), gv[:, :, OWN:EXT].reshape(D, EXT - OWN)],
@@ -454,19 +508,8 @@
         def _():
             grad_copy(index, side).start()
 
-    attended = att[...].reshape(D, OWN).T
-    out_rows = (x_rows.astype(F32) + dot_nt(attended, wout[...])).astype(BF16)
-    out_send[...] = moved(gather_rows(token_row), out_rows).reshape(8, 16, D)
-
-    def out_copy(k, carry):
-        to = (gy + k) & (GY - 1)
-        remote(
-            out_send.at[to], out_stage.at[gy], o_ssem.at[0], o_rsem.at[0], (gx, to)
-        ).start()
-        return carry
-
-    lax.fori_loop(1, GY, out_copy, 0)
-    out_stage[gy] = out_send[gy]
+    wait_for(out_stage.at[pl.ds(0, GY - 1)], o_rsem.at[0])
+    out[...] = moved(scatter_rows(natural_row), out_stage[...].reshape(OWN, D))
 
     def line_sum(own, others, me):
         ry_ = own.astype(F32)
@@ -474,71 +517,56 @@
             ry_ = ry_ + others[(me + k) & 3].astype(F32)
         return ry_.astype(BF16)
 
-    wait_for(rx.at[pl.ds(0, 3)], a_rsem.at[0])
-    total = line_sum(sx[at_x], rx, at_x)
-    for slot in range(2):
-        for z in range(4):
-            tx[z, slot] = total[slot, z]
-
-    for y in range(2):
-        def send_tx(k, carry):
-            z = (at_z + k) & 3
+    @pl.when(at_y < 3)
+    def _():
+        wait_for(ry.at[pl.ds(0, 3)], a_rsem.at[1])
+        ty[...] = line_sum(sy[at_y], ry, at_y)
+
+        def send_ty(k, carry):
+            x, z = (at_x + (k >> 2)) & 3, (at_z + k) & 3
             remote(
-                tx.at[z, y], fx.at[at_y * 4 + at_z],
-                b_ssem.at[0], b_rsem.at[0], device_at(y, at_x, z),
+                ty.at[x, z], fy.at[at_x * 4 + at_z], b_ssem.at[0], b_rsem.at[0],
+                device_at(at_y, x, z),
             ).start()
             return carry
 
-        lax.fori_loop(1, 4, send_tx, 0)
-
-        @pl.when(at_y != y)
-        def _():
-            send_tx(0, 0)
-
-        @pl.when(at_y == y)
-        def _():
-            fx[at_y * 4 + at_z] = tx[at_z, y]
-
-    wait_for(rz.at[pl.ds(0, 3)], a_rsem.at[2])
-    total = line_sum(sz[at_z], rz, at_z)
-    for slot in range(6):
-        for x in range(4):
-            tz[x, slot] = total[slot, x]
-
-    for y in range(4):
-        first, count = SPAN_Z[y]
-
-        def send_tz(k, carry):
-            x = (at_x + k) & 3
-            remote(
-                tz.at[x, pl.ds(first, count)], fz.at[at_y * 4 + at_x, pl.ds(0, count)],
-                b_ssem.at[0], b_rsem.at[0], device_at(y, x, at_z),
-            ).start()
-            return carry
-
-        lax.fori_loop(1, 4, send_tz, 0)
-
-        @pl.when(at_y != y)
-        def _():
-            send_tz(0, 0)
-
-        @pl.when(at_y == y)
-        def _():
-            fz[at_y * 4 + at_x, 0:count] = tz[at_x, first : first + count]
-
-    wait_for(ry.at[pl.ds(0, 3)], a_rsem.at[1])
-    ty[...] = line_sum(sy[at_y], ry, at_y)
-
-    def send_ty(k, carry):
-        x, z = (at_x + (k >> 2)) & 3, (at_z + k) & 3
-        remote(
-            ty.at[x, z], fy.at[at_x * 4 + at_z], b_ssem.at[0], b_rsem.at[0],
-            device_at(at_y, x, z),
-        ).start()
-        return carry
-
-    lax.fori_loop(1, 16, send_ty, 0)
-    fy[at_x * 4 + at_z] = ty[at_x, at_z]
+        lax.fori_loop(1, 16, send_ty, 0)
+        fy[at_x * 4 + at_z] = ty[at_x, at_z]
+
+    def second_step(line, own, others, me, sums, spans, landing, sem, target):
+        wait_for(others.at[pl.ds(0, 3)], sem)
+        total = line_sum(own[me], others, me)
+        for slot in range(total.shape[0]):
+            for at in range(4):
+                sums[at, slot] = total[slot, at]
+        for y in range(4):
+            first, count = spans[y]
+
+            def send(k, carry):
+                to = (line + k) & 3
+                remote(
+                    sums.at[to, pl.ds(first, count)],
+                    landing.at[at_y * 4 + line, pl.ds(0, count)],
+                    b_ssem.at[0], b_rsem.at[0], target(y, to),
+                ).start()
+                return carry
+
+            lax.fori_loop(1, 4, send, 0)
+
+            @pl.when(at_y != y)
+            def _():
+                send(0, 0)
+
+            @pl.when(at_y == y)
+            def _():
+                landing[at_y * 4 + line, 0:count] = sums[line, first : first + count]
+
+    second_step(
+        at_z, sx, rx, at_x, tx, SPAN_X, fx, a_rsem.at[0], lambda y, z: device_at(y, at_x, z)
+    )
+    second_step(
+        at_x, sz, rz, at_z, tz, SPAN_Z, fz, a_rsem.at[2], lambda y, x: device_at(y, x, at_z)
+    )
 
     grad_own = jnp.concatenate(
         [
@@ -574,30 +602,36 @@
         )
     grad_n = jnp.concatenate(planes, axis=0).reshape(OWN, D)
     x_float = x_rows.astype(F32)
-    inverse = lax.rsqrt(jnp.mean(x_float * x_float, axis=-1, keepdims=True) + EPSILON)
-    x_hat = x_float * inverse
-    grad_x = inverse * (grad_n - x_hat * jnp.mean(grad_n * x_hat, axis=-1, keepdims=True))
+    x_inv = lax.rsqrt(jnp.mean(x_float * x_float, axis=-1, keepdims=True) + EPSILON)
+    x_hat = x_float * x_inv
+    grad_x = x_inv * (grad_n - x_hat * jnp.mean(grad_n * x_hat, axis=-1, keepdims=True))
     grad_rows = (cot_tok[...].astype(F32) + grad_x).astype(BF16)
     gin[...] = moved(scatter_rows(slab_row), grad_rows)
 
-    wait_for(out_stage.at[pl.ds(0, GY - 1)], o_rsem.at[0])
-    out[...] = moved(scatter_rows(natural_row), out_stage[...].reshape(OWN, D))
-
     wait_for(rz.at[pl.ds(0, 3), pl.ds(0, 5)], b_rsem.at[0])
 
-    def owned(blocks):
-        return jnp.sum(blocks.astype(F32), axis=0) * FACTOR
-
-    gw[:, 0:256] = owned(fy[...])
-    gw[:, 256:384] = owned(fz[:, 0])
-
-    @pl.when(at_y < 2)
+    def put(tile, blocks):
+        gw[:, 128 * tile : 128 * tile + 128] = jnp.sum(blocks.astype(F32), axis=0) * FACTOR
+
+    @pl.when(at_y < 3)
     def _():
-        gw[:, 384:512] = owned(fx[...])
-
-    @pl.when(at_y >= 2)
+        put(0, fy[...])
+        put(1, fx[:, 0])
+
+    @pl.when(at_y == 3)
     def _():
-        gw[:, 384:512] = owned(fz[:, 1])
+        put(0, fx[:, 0])
+        put(1, fx[:, 1])
+
+    put(2, fz[:, 0])
+
+    @pl.when(at_y == 0)
+    def _():
+        put(3, fx[:, 1])
+
+    @pl.when(at_y > 0)
+    def _():
+        put(3, fz[:, 1])
 
     for index, side in enumerate(SIDES):
         @pl.when(exists(side))
@@ -610,9 +644,17 @@
     wait_for(cot_send.at[pl.ds(0, GY - 1)], c_ssem.at[0])
     wait_for(out_send.at[pl.ds(0, GY - 1)], o_ssem.at[0])
     wait_for(rx.at[pl.ds(0, 3)], a_ssem.at[0])
-    wait_for(ry.at[pl.ds(0, 3)], a_ssem.at[1])
     wait_for(rz.at[pl.ds(0, 3)], a_ssem.at[2])
-    wait_for(rz.at[pl.ds(0, 3), pl.ds(0, 5)], b_ssem.at[0])
+
+    @pl.when(at_y < 3)
+    def _():
+        wait_for(ry.at[pl.ds(0, 2)], a_ssem.at[1])
+        wait_for(rz.at[pl.ds(0, 4), pl.ds(0, 4)], b_ssem.at[0])
+
+    @pl.when(at_y == 3)
+    def _():
+        wait_for(ry.at[pl.ds(0, 3)], a_ssem.at[1])
+        wait_for(rz.at[pl.ds(0, 3), pl.ds(0, 4)], b_ssem.at[0])
 
 
 def placed(out, gin, gw, out_at, gin_at, gw_at):
@@ -659,6 +701,9 @@
             pltpu.VMEM((4, 128, OWN), BF16),
             pltpu.VMEM((4, EXT, 2 * OWN), F32),
             pltpu.VMEM((4, EXT, 2 * OWN), BF16),
+            pltpu.VMEM((4, 1, 2 * OWN), F32),
+            pltpu.VMEM((2, EXT, 2 * OWN), F32),
+            pltpu.VMEM((2, EXT, 2 * OWN), BF16),
             pltpu.VMEM((4, 128, OWN), BF16),
             pltpu.VMEM((4, 128, EXT), BF16),
             pltpu.VMEM((4, 128, EXT), BF16),
@@ -667,17 +712,17 @@
             pltpu.VMEM((EXT, 2 * OWN), F32),
             pltpu.VMEM((4, 2, 128, D), BF16),
             pltpu.VMEM((4, 2, 128, D), BF16),
-            pltpu.VMEM((4, 2, 4, 16, 128), BF16),
-            pltpu.VMEM((4, 4, 4, 16, 256), BF16),
             pltpu.VMEM((4, 6, 4, 16, 128), BF16),
-            pltpu.VMEM((4, 2, 4, 16, 128), BF16),
-            pltpu.VMEM((4, 4, 4, 16, 256), BF16),
+            pltpu.VMEM((3, 4, 4, 16, 128), BF16),
+            pltpu.VMEM((4, 7, 4, 16, 128), BF16),
             pltpu.VMEM((4, 6, 4, 16, 128), BF16),
-            pltpu.VMEM((4, 2, 16, 128), BF16),
-            pltpu.VMEM((4, 4, 16, 256), BF16),
+            pltpu.VMEM((4, 4, 4, 16, 128), BF16),
+            pltpu.VMEM((4, 7, 4, 16, 128), BF16),
             pltpu.VMEM((4, 6, 16, 128), BF16),
+            pltpu.VMEM((4, 4, 16, 128), BF16),
+            pltpu.VMEM((4, 7, 16, 128), BF16),
+            pltpu.VMEM((16, 2, 16, 128), BF16),
             pltpu.VMEM((16, 16, 128), BF16),
-            pltpu.VMEM((16, 16, 256), BF16),
             pltpu.VMEM((16, 2, 16, 128), BF16),
             pltpu.VMEM((16, 16, D), BF16),
             pltpu.VMEM((16, 16, D), BF16),

time: 37 us -> 34.6 us (0.935)
  Pallas kernels: 36.2 us -> 33.8 us
    pallas_call x1, Pallas kernels: 35.5 us -> 33.1 us  [on_device(): pl.pallas_call(kernel, out_shape=(pltpu.VMEM((OWN, D), BF16), pltpu.VMEM(...]
where the time goes in v4:
time: 34.6 us; the launch traced here: 34.4 us
  Pallas kernels  33.8 us (98%)
  between operations  0.64 us (2%)
    pallas_call x1, Pallas kernels, on_device(): pl.pallas_call(kernel, out_shape=(pltpu.VMEM((OWN, D), BF16), pltpu.VMEM(...  33.1 us
    pallas_call x1, Pallas kernels, on_device(): pl.pallas_call(placed, out_shape=(jax.ShapeDtypeStruct((OWN, D), BF16), j...  0.72 us

profile of v4, /device:TPU:0, one launch (start us, length us, event | category | flops | bytes accessed | tf_op | source)
XLA Modules:
  0.0 34.4 jit_solution(9865088945595133938)
XLA Ops:
  0.6 33.1 %shard_map.76 = (bf16[128,512]{1,0:T(8,128)(2,1)S(1)}, bf16[128,512]{1,0:T(8,128)(2,1)S(1)}, f32[16,512]{1,0:T(8,128)S(1)}) custom-call(bf16[2,16,4,512]{3,2,1,0:T(4,128)(2,1)} %slab_hbm.1, bf16[128,512]{1,0:T(8,128)(2,1)} %bitcast.2, bf16[1536,512]{1,0:T(8,128)(2,1)} %wqkv_hbm.1, bf16[512,512]{1,0:T(8,128)(2,1)} %wout_hbm.1, f32[8]{0:T(128)} %scale_hbm.1), custom_call_target="tpu_custom_call" | custom-call | tf_op jit(solution)/shard_map/pallas_call | solution.py:670
  33.7 0.7 %shard_map.77 = (bf16[128,512]{1,0:T(8,128)(2,1)}, bf16[2,16,4,512]{3,2,1,0:T(4,128)(2,1)}, f32[16,512]{1,0:T(8,128)}) custom-call(bf16[128,512]{1,0:T(8,128)(2,1)S(1)} %get-tuple-element.9.out, bf16[128,512]{1,0:T(8,128)(2,1)S(1)} %get-tuple-element.10.gin, f32[16,512]{1,0:T(8,128)S(1)} %get-tuple-element.11.gw), custom_call_target="tpu_custom_call" | custom-call | tf_op jit(solution)/shard_map/pallas_call | solution.py:744

commit v5 on v4

--- a/solution.py
+++ b/solution.py
@@ -157,8 +157,8 @@
 
         return carry
 
-    lax.fori_loop(1, 16, greet_plane, 0)
-    lax.fori_loop(0, 12, greet_lines, 0)
+    lax.fori_loop(1, 16, greet_plane, 0, unroll=15)
+    lax.fori_loop(0, 12, greet_lines, 0, unroll=12)
 
     load_slab.wait()
     slab_rows = slab[...].astype(F32).reshape(OWN, D).astype(BF16)
@@ -437,7 +437,8 @@
             ).start()
             return carry
 
-        lax.fori_loop(1, 4, step, 0)
+        for k in range(1, 4):
+            step(k, 0)
 
     def send_y(part):
         @pl.when(at_y != part)
@@ -482,10 +483,10 @@
     sum_own(3)
     send_lines(pl.ds(4, 2), pl.ds(5, 2))
     backward_pairs(core, 2 + core)
-    for part in range(3):
+    for part in (0, 2, 1):
         sum_own(part)
         send_y(part)
-    send_lines(pl.ds(0, 4), pl.ds(0, 5))
+        send_lines(pl.ds(*SPAN_X[part]), pl.ds(*SPAN_Z[part]))
 
     grad_kv_halo = jnp.concatenate(
         [gk[:, :, OWN:EXT].reshape(D, EXT - OWN), gv[:, :, OWN:EXT].reshape(D, EXT - OWN)],
@@ -510,63 +511,6 @@
 
     wait_for(out_stage.at[pl.ds(0, GY - 1)], o_rsem.at[0])
     out[...] = moved(scatter_rows(natural_row), out_stage[...].reshape(OWN, D))
-
-    def line_sum(own, others, me):
-        ry_ = own.astype(F32)
-        for k in range(1, 4):
-            ry_ = ry_ + others[(me + k) & 3].astype(F32)
-        return ry_.astype(BF16)
-
-    @pl.when(at_y < 3)
-    def _():
-        wait_for(ry.at[pl.ds(0, 3)], a_rsem.at[1])
-        ty[...] = line_sum(sy[at_y], ry, at_y)
-
-        def send_ty(k, carry):
-            x, z = (at_x + (k >> 2)) & 3, (at_z + k) & 3
-            remote(
-                ty.at[x, z], fy.at[at_x * 4 + at_z], b_ssem.at[0], b_rsem.at[0],
-                device_at(at_y, x, z),
-            ).start()
-            return carry
-
-        lax.fori_loop(1, 16, send_ty, 0)
-        fy[at_x * 4 + at_z] = ty[at_x, at_z]
-
-    def second_step(line, own, others, me, sums, spans, landing, sem, target):
-        wait_for(others.at[pl.ds(0, 3)], sem)
-        total = line_sum(own[me], others, me)
-        for slot in range(total.shape[0]):
-            for at in range(4):
-                sums[at, slot] = total[slot, at]
-        for y in range(4):
-            first, count = spans[y]
-
-            def send(k, carry):
-                to = (line + k) & 3
-                remote(
-                    sums.at[to, pl.ds(first, count)],
-                    landing.at[at_y * 4 + line, pl.ds(0, count)],
-                    b_ssem.at[0], b_rsem.at[0], target(y, to),
-                ).start()
-                return carry
-
-            lax.fori_loop(1, 4, send, 0)
-
-            @pl.when(at_y != y)
-            def _():
-                send(0, 0)
-
-            @pl.when(at_y == y)
-            def _():
-                landing[at_y * 4 + line, 0:count] = sums[line, first : first + count]
-
-    second_step(
-        at_z, sx, rx, at_x, tx, SPAN_X, fx, a_rsem.at[0], lambda y, z: device_at(y, at_x, z)
-    )
-    second_step(
-        at_x, sz, rz, at_z, tz, SPAN_Z, fz, a_rsem.at[2], lambda y, x: device_at(y, x, at_z)
-    )
 
     grad_own = jnp.concatenate(
         [
@@ -577,6 +521,64 @@
         axis=0,
     )
     grad_n = dot_tn(grad_own, wqkv[...]).reshape(2, 4, 16, D)
+    def line_sum(own, others, me):
+        ry_ = own.astype(F32)
+        for k in range(1, 4):
+            ry_ = ry_ + others[(me + k) & 3].astype(F32)
+        return ry_.astype(BF16)
+
+    @pl.when(at_y < 3)
+    def _():
+        wait_for(ry.at[pl.ds(0, 3)], a_rsem.at[1])
+        ty[...] = line_sum(sy[at_y], ry, at_y)
+
+        def send_ty(k, carry):
+            x, z = (at_x + (k >> 2)) & 3, (at_z + k) & 3
+            remote(
+                ty.at[x, z], fy.at[at_x * 4 + at_z], b_ssem.at[0], b_rsem.at[0],
+                device_at(at_y, x, z),
+            ).start()
+            return carry
+
+        lax.fori_loop(1, 16, send_ty, 0, unroll=5)
+        fy[at_x * 4 + at_z] = ty[at_x, at_z]
+
+    def second_step(line, own, others, me, sums, spans, landing, sem, target):
+        wait_for(others.at[pl.ds(0, 3)], sem)
+        total = line_sum(own[me], others, me)
+        for slot in range(total.shape[0]):
+            for at in range(4):
+                sums[at, slot] = total[slot, at]
+        for y in range(4):
+            first, count = spans[y]
+
+            def send(k, carry):
+                to = (line + k) & 3
+                remote(
+                    sums.at[to, pl.ds(first, count)],
+                    landing.at[at_y * 4 + line, pl.ds(0, count)],
+                    b_ssem.at[0], b_rsem.at[0], target(y, to),
+                ).start()
+                return carry
+
+            for k in range(1, 4):
+                send(k, 0)
+
+            @pl.when(at_y != y)
+            def _():
+                send(0, 0)
+
+            @pl.when(at_y == y)
+            def _():
+                landing[at_y * 4 + line, 0:count] = sums[line, first : first + count]
+
+    second_step(
+        at_z, sx, rx, at_x, tx, SPAN_X, fx, a_rsem.at[0], lambda y, z: device_at(y, at_x, z)
+    )
+    second_step(
+        at_x, sz, rz, at_z, tz, SPAN_Z, fz, a_rsem.at[2], lambda y, x: device_at(y, x, at_z)
+    )
+
     for index, side in enumerate(SIDES):
         opposite = SIDES.index((-side[0], -side[1]))
         start, size = REGION[side]

time: 34.6 us -> 33.8 us (0.977)
  Pallas kernels: 33.8 us -> 33 us
    pallas_call x1, Pallas kernels: 33.1 us -> 32.3 us  [on_device(): pl.pallas_call(kernel, out_shape=(pltpu.VMEM((OWN, D), BF16), pltpu.VMEM(...]
where the time goes in v5:
time: 33.8 us; the launch traced here: 33.6 us
  Pallas kernels  33 us (98%)
  between operations  0.64 us (2%)
    pallas_call x1, Pallas kernels, on_device(): pl.pallas_call(kernel, out_shape=(pltpu.VMEM((OWN, D), BF16), pltpu.VMEM(...  32.3 us
    pallas_call x1, Pallas kernels, on_device(): pl.pallas_call(placed, out_shape=(jax.ShapeDtypeStruct((OWN, D), BF16), j...  0.72 us

profile of v5, /device:TPU:0, one launch (start us, length us, event | category | flops | bytes accessed | tf_op | source)
XLA Modules:
  0.0 33.6 jit_solution(3835473126069338813)
XLA Ops:
  0.6 32.3 %shard_map.76 = (bf16[128,512]{1,0:T(8,128)(2,1)S(1)}, bf16[128,512]{1,0:T(8,128)(2,1)S(1)}, f32[16,512]{1,0:T(8,128)S(1)}) custom-call(bf16[2,16,4,512]{3,2,1,0:T(4,128)(2,1)} %slab_hbm.1, bf16[128,512]{1,0:T(8,128)(2,1)} %bitcast.2, bf16[1536,512]{1,0:T(8,128)(2,1)} %wqkv_hbm.1, bf16[512,512]{1,0:T(8,128)(2,1)} %wout_hbm.1, f32[8]{0:T(128)} %scale_hbm.1), custom_call_target="tpu_custom_call" | custom-call | tf_op jit(solution)/shard_map/pallas_call | solution.py:672
  32.9 0.7 %shard_map.77 = (bf16[128,512]{1,0:T(8,128)(2,1)}, bf16[2,16,4,512]{3,2,1,0:T(4,128)(2,1)}, f32[16,512]{1,0:T(8,128)}) custom-call(bf16[128,512]{1,0:T(8,128)(2,1)S(1)} %get-tuple-element.9.out, bf16[128,512]{1,0:T(8,128)(2,1)S(1)} %get-tuple-element.10.gin, f32[16,512]{1,0:T(8,128)S(1)} %get-tuple-element.11.gw), custom_call_target="tpu_custom_call" | custom-call | tf_op jit(solution)/shard_map/pallas_call | solution.py:746
